TPU v7x, 32 devices: a whole 2x2x4 slice. The times are simulated.
32 devices in a mesh: groups: 1, ctx: 16 (over z, y, core), uly: 2 (over x), rep: 1.
Axes of the slice: x: 2, y: 2, z: 4, core: 2. Of those that a mesh axis runs over, the one named last changes fastest.
Arguments:
- q_proj: bfloat16 [4096, 5120], P(('groups', 'ctx', 'rep', 'uly')), may hold values from -8 to 8
- k_proj: bfloat16 [4096, 5120], P(('groups', 'ctx', 'rep', 'uly')), may hold values from -8 to 8
- v_proj: bfloat16 [4096, 5120], P(('groups', 'ctx', 'rep', 'uly')), may hold values from -4 to 4
- kv_list: int32 [32, 16], P('groups'), may hold values from -1 to 31, as said below
Outputs:
- attended: bfloat16 [4096, 5120], P(('groups', 'ctx', 'rep', 'uly'))
Inputs may be any that keep to these rules, and one draw needn't show every extreme that they name: `kv_list`: frame f holds blocks f * 2 to (f + 1) * 2 - 1. Row i lists, in ascending order and padded with -1 at the end, the key blocks that query block i attends: all 2 blocks of its own frame and some blocks of frames at distance 1 to 7. For a query frame f and a distance d whose frame f + d exists, the blocks of frame f + d listed by the query blocks of f are exactly 1 distinct blocks if |d| = 1 and exactly one block if 2 <= |d| <= 7; up to |d| = 3 every query block of f lists all of them.
All inputs are finite; a program needn't handle non-finite values.
Results may differ from a plain program's by a relative error of at most 0.014.
Values may be sent and summed in bfloat16 or wider, within the bound.
No kernel may reach another device: no remote copies, remote signals or barrier semaphores. Data moves between devices by JAX's collectives and lax.ppermute only.
A program may use at most 128 MiB of HBM per device.

v0:
```python
import functools
import math

import jax
import jax.numpy as jnp
from jax import lax
from jax.experimental import pallas as pl
from jax.experimental.pallas import tpu as pltpu
from jax.sharding import Mesh, PartitionSpec as P

HD = 128
BLK = 128
BPF = 2
REACH = 7
CHUNKS = (2, 3)
PACK_VMEM = 60 * 1024 * 1024
NEAR_VMEM = 24 * 1024 * 1024
OTHER_VMEM = 14 * 1024 * 1024
little = dict(flops=1024, bytes_accessed=1024, transcendentals=0)
some = dict(flops=20_000_000_000, bytes_accessed=1024, transcendentals=0)
much = dict(flops=100_000_000_000, bytes_accessed=1024, transcendentals=0)

very_low = -1e30
to_log2 = math.log2(math.e) * HD ** -0.5


def staged_copies(steps, sems):
    count = len(steps)
    fetches = [pltpu.make_async_copy(s, stage, sems.at[i]) for i, (s, stage, t) in enumerate(steps)]
    puts = [pltpu.make_async_copy(stage, t, sems.at[count + i]) for i, (s, stage, t) in enumerate(steps)]
    for fetch in fetches:
        fetch.start()
    for fetch, put in zip(fetches, puts):
        fetch.wait()
        put.start()
    for put in puts:
        put.wait()


anywhere = pl.BlockSpec(memory_space=pl.ANY)
in_hbm = pl.BlockSpec(memory_space=pltpu.HBM)
in_vmem = pl.BlockSpec(memory_space=pltpu.VMEM)


def copy_call(plan, shapes, count, operands, scalars=(), after=(), cost=little):
    def body(*refs):
        first = len(scalars)
        last = first + len(operands)
        results = refs[last + len(after) :]
        n = len(shapes)
        staged_copies(plan(refs[:first], refs[first:last], results[:n], results[n : 2 * n]), results[2 * n])

    return pl.pallas_call(
        body,
        out_shape=shapes,
        in_specs=[pl.BlockSpec(memory_space=pltpu.SMEM)] * len(scalars) + [anywhere] * (len(operands) + len(after)),
        out_specs=[anywhere] * len(shapes),
        scratch_shapes=[pltpu.VMEM(s.shape, s.dtype) for s in shapes] + [pltpu.SemaphoreType.DMA((2 * count,))],
        compiler_params=pltpu.CompilerParams(vmem_limit_bytes=OTHER_VMEM),
        cost_estimate=pl.CostEstimate(**cost),
    )(*scalars, *operands, *after)


def pack(arrays, starts, widths, team_size, after=()):
    rows = arrays[0].shape[0]
    lows = [sum(widths[:i]) for i in range(len(widths))]
    count = len(arrays) * len(starts)

    def body(*refs):
        sources = refs[: len(arrays)]
        out, *stages, sems = refs[len(arrays) + len(after) :]
        fetches, puts = [], []
        for kind, source in enumerate(sources):
            for number, (start, width, low) in enumerate(zip(starts, widths, lows)):
                stage = stages[number].at[kind]
                place = len(fetches)
                columns = pl.ds(start, team_size * width)
                fetches.append(pltpu.make_async_copy(source.at[:, columns], stage, sems.at[place, team_size]))
                puts.append(
                    [
                        pltpu.make_async_copy(
                            stage.at[:, pl.ds(member * width, width)],
                            out.at[member, kind, :, pl.ds(low, width)],
                            sems.at[place, member],
                        )
                        for member in range(team_size)
                    ]
                )
        for fetch in fetches:
            fetch.start()
        for fetch, some_puts in zip(fetches, puts):
            fetch.wait()
            for put in some_puts:
                put.start()
        for some_puts in puts:
            for put in some_puts:
                put.wait()

    return pl.pallas_call(
        body,
        out_shape=jax.ShapeDtypeStruct((team_size, len(arrays), rows, sum(widths)), jnp.bfloat16),
        in_specs=[anywhere] * (len(arrays) + len(after)),
        out_specs=anywhere,
        scratch_shapes=[
            *[pltpu.VMEM((len(arrays), rows, team_size * width), jnp.bfloat16) for width in widths],
            pltpu.SemaphoreType.DMA((count, team_size + 1)),
        ],
        compiler_params=pltpu.CompilerParams(vmem_limit_bytes=PACK_VMEM),
        cost_estimate=pl.CostEstimate(**some),
    )(*arrays, *after)


def unpack(parts, starts, model_width):
    members, rows, _ = parts[0].shape
    count = members * len(parts)

    def body(*refs):
        *sources, out, sems = refs
        puts = []
        for start, source in zip(starts, sources):
            width = source.shape[2]
            for member in range(members):
                columns = pl.ds(start + member * width, width)
                puts.append(pltpu.make_async_copy(source.at[member], out.at[:, columns], sems.at[len(puts)]))
                puts[-1].start()
        for put in puts:
            put.wait()

    return pl.pallas_call(
        body,
        out_shape=jax.ShapeDtypeStruct((rows, model_width), jnp.bfloat16),
        in_specs=[pl.BlockSpec(memory_space=pltpu.VMEM)] * len(parts),
        out_specs=in_hbm,
        scratch_shapes=[pltpu.SemaphoreType.DMA((count,))],
        compiler_params=pltpu.CompilerParams(vmem_limit_bytes=8 * 1024 * 1024),
        cost_estimate=pl.CostEstimate(**little),
    )(*parts)


def select(held, places, count, whole, after=()):
    def plan(scalars, sources, outs, stages):
        (place_ref,) = scalars
        steps = []
        for side, (source, stage, out) in enumerate(zip(sources, stages, outs)):
            one = pl.ds(0 if side == 0 else whole, count)
            steps.append((source.at[pl.ds(place_ref[side], count)], stage.at[one], out.at[one]))
            if whole > 0:
                rest = pl.ds(count if side == 0 else 0, whole)
                kept = pl.ds(source.shape[0] - whole if side == 0 else 0, whole)
                steps.append((source.at[kept], stage.at[rest], out.at[rest]))
        return steps

    shapes = [jax.ShapeDtypeStruct((count + whole,) + array.shape[1:], array.dtype) for array in held]
    return copy_call(plan, shapes, 2 * (2 if whole > 0 else 1), held, scalars=[places], after=after, cost=much)


def columns_of(head):
    return pl.ds(pl.multiple_of(head * HD, HD), HD)


def flat(rows):
    return rows.reshape(rows.shape[0] * rows.shape[1], HD)


def masked_scores(queries, keys, masks):
    tiles = [[] for _ in range(BPF)]
    for first in range(0, len(keys), 2):
        some = jnp.concatenate(keys[first : first + 2], axis=0)
        scores = lax.dot_general(queries, some, (((1,), (1,)), ((), ())), preferred_element_type=jnp.float32)
        for side, mask in enumerate(masks[first : first + 2]):
            for b in range(BPF):
                tile = scores[b * BLK : (b + 1) * BLK, side * BLK : (side + 1) * BLK]
                tiles[b].append(tile if mask is None else tile + mask[b])
    return tiles


def largest(tiles):
    return jnp.max(functools.reduce(jnp.maximum, tiles), axis=1, keepdims=True)


def weighted(tiles, tops, values):
    totals, weights = [], []
    for b in range(BPF):
        exps = [jnp.exp2((tile - tops[b]) * to_log2) for tile in tiles[b]]
        totals.append(jnp.sum(functools.reduce(jnp.add, exps), axis=1, keepdims=True))
        weights.append(jnp.concatenate([e.astype(jnp.bfloat16) for e in exps], axis=1))
    mixed = jnp.dot(
        jnp.concatenate(weights, axis=0), jnp.concatenate(values, axis=0), preferred_element_type=jnp.float32
    )
    return mixed, jnp.concatenate(totals, axis=0)


def mask_of(codes):
    return [jnp.where(code > 0, 0.0, very_low).astype(jnp.float32) for code in codes]


def each_head(heads, fetches, puts, work):
    for head in range(heads):
        for fetch in fetches(head):
            fetch.start()

    def one_head(head, carry):
        for fetch in fetches(head):
            fetch.wait()
        work(head)
        for put in puts(head):
            put.start()
        return carry

    lax.fori_loop(0, heads, one_head, 0)
    for head in range(heads):
        for put in puts(head):
            put.wait()


def near_kernel(frames, near, pieces_of, heads, first_head, code_ref, q_hbm, *refs):
    *piece_refs, acc_ref, top_ref, total_ref, q_ref, store, sems = refs
    per_frame = BPF * pieces_of
    width = frames + 2 * REACH

    def fetches(head):
        columns = columns_of(head)
        found = [(q_hbm.at[:, 0, :, columns_of(head + first_head)], q_ref.at[:, :, columns])]
        start = 0
        for piece in piece_refs:
            size = piece.shape[0]
            found.append((piece.at[:, :, :, columns], store.at[pl.ds(start, size), :, :, columns]))
            start += size
        return [pltpu.make_async_copy(a, b, sems.at[head, i]) for i, (a, b) in enumerate(found)]

    def item(frame, head):
        columns = columns_of(head)
        own = (frame + near) * BPF * pieces_of
        keys, values, masks = [], [], []
        for b in range(BPF):
            keys.append(flat(store[pl.ds(own + b * pieces_of, pieces_of), 0, :, columns]))
            values.append(flat(store[pl.ds(own + b * pieces_of, pieces_of), 1, :, columns]))
            masks.append(None)
        for other in range(frames + 2 * near - 1):
            relative = other - near
            relative = relative + jnp.where(relative >= frame, 1, 0)
            codes = [code_ref[(frame * BPF + b) * width + relative + REACH] for b in range(BPF)]
            pick = jnp.maximum(codes[0], codes[1]) // 2
            place = ((relative + near) * BPF + pick) * pieces_of
            keys.append(flat(store[pl.ds(place, pieces_of), 0, :, columns]))
            values.append(flat(store[pl.ds(place, pieces_of), 1, :, columns]))
            masks.append(mask_of(codes))
        queries = flat(q_ref[pl.ds(frame * per_frame, per_frame), :, columns])
        tiles = masked_scores(queries, keys, masks)
        tops = [largest(tiles[b]) for b in range(BPF)]
        mixed, totals = weighted(tiles, tops, values)
        acc_ref[head, frame] = mixed
        top_ref[head, frame] = jnp.broadcast_to(jnp.concatenate(tops, axis=0), mixed.shape)
        total_ref[head, frame] = jnp.broadcast_to(totals, mixed.shape)

    together = 2 if frames % 2 == 0 else 1

    def work(head):
        def step(index, carry):
            for offset in range(together):
                item(index * together + offset, head)
            return carry

        lax.fori_loop(0, frames // together, step, 0)

    each_head(heads, fetches, lambda head: [], work)


def far_kernel(frames, near, pieces_of, heads, first_head, code_ref, q_hbm, *refs):
    left_hbm, right_hbm, acc_ref, top_ref, total_ref, out_hbm, token, q_ref, left, right, out_ref, sems, put_sems = refs
    token[...] = jnp.zeros_like(token)
    per_frame = BPF * pieces_of
    width = frames + 2 * REACH

    def fetches(head):
        columns = columns_of(head)
        pairs = [
            (q_hbm.at[:, 0, :, columns_of(head + first_head)], q_ref.at[:, :, columns]),
            (left_hbm.at[:, :, :, columns], left.at[:, :, :, columns]),
            (right_hbm.at[:, :, :, columns], right.at[:, :, :, columns]),
        ]
        return [pltpu.make_async_copy(a, b, sems.at[head, i]) for i, (a, b) in enumerate(pairs)]

    def puts(head):
        columns = columns_of(head)
        return [pltpu.make_async_copy(out_ref.at[:, :, columns], out_hbm.at[:, :, columns], put_sems.at[head])]

    def item(frame, head):
        columns = columns_of(head)
        keys, values, masks = [], [], []
        for relative in [*range(-REACH, -near), *range(frames + near, frames + REACH)]:
            if abs(relative - frame) > REACH:
                continue
            codes = [code_ref[(frame * BPF + b) * width + relative + REACH] for b in range(BPF)]
            pick = jnp.maximum(codes[0], codes[1]) // 2
            if relative < 0:
                piece, place = left, (0 if relative == -REACH else (relative + REACH) * BPF - 1 + pick)
            else:
                first = (relative - frames - near) * BPF
                piece, place = right, (first if relative == frames + REACH - 1 else first + pick)
            keys.append(flat(piece[pl.ds(place * pieces_of, pieces_of), 0, :, columns]))
            values.append(flat(piece[pl.ds(place * pieces_of, pieces_of), 1, :, columns]))
            masks.append(mask_of(codes))
        queries = flat(q_ref[pl.ds(frame * per_frame, per_frame), :, columns])
        tiles = masked_scores(queries, keys, masks)
        near_top = top_ref[head, frame]
        tops = [jnp.maximum(largest(tiles[b]), near_top[b * BLK : (b + 1) * BLK]) for b in range(BPF)]
        mixed, totals = weighted(tiles, tops, values)
        shrink = jnp.exp2((near_top - jnp.concatenate(tops, axis=0)) * to_log2)
        result = (acc_ref[head, frame] * shrink + mixed) / (total_ref[head, frame] * shrink + totals)
        out_ref[pl.ds(frame * per_frame, per_frame), :, columns] = result.astype(jnp.bfloat16).reshape(
            per_frame, BLK // pieces_of, HD
        )

    def work(head):
        for frame in range(frames):
            item(frame, head)

    each_head(heads, fetches, puts, work)


def measured_cost(blocks):
    return dict(flops=6 * blocks * BPF * 4 * BLK * BLK * HD, bytes_accessed=1024, transcendentals=0)


def attend_near(codes, queries, pieces, frames, near, first_head, cost=None, after=()):
    members, _, rows, _ = queries.shape
    pieces_of = BLK // rows
    width = pieces[0].shape[3]
    heads = width // HD
    stored = sum(piece.shape[0] for piece in pieces)

    def body(code_ref, q_hbm, *refs):
        kept = refs[: len(pieces)] + refs[len(pieces) + len(after) :]
        near_kernel(frames, near, pieces_of, heads, first_head, code_ref, q_hbm, *kept)

    partial = jax.ShapeDtypeStruct((heads, frames, BPF * BLK, HD), jnp.float32)
    return pl.pallas_call(
        body,
        out_shape=[partial] * 3,
        in_specs=[pl.BlockSpec(memory_space=pltpu.SMEM)] + [anywhere] * (1 + len(pieces) + len(after)),
        out_specs=[in_vmem] * 3,
        scratch_shapes=[
            pltpu.VMEM((members, rows, width), jnp.bfloat16),
            pltpu.VMEM((stored, 2, rows, width), jnp.bfloat16),
            pltpu.SemaphoreType.DMA((heads, 1 + len(pieces))),
        ],
        compiler_params=pltpu.CompilerParams(vmem_limit_bytes=NEAR_VMEM),
        cost_estimate=pl.CostEstimate(**(cost or measured_cost(frames * heads * (frames + 2 * near + 1)))),
    )(codes, queries, *pieces, *after)


def attend_far(codes, queries, far, partials, frames, near, first_head, cost=None, after=()):
    members, _, rows, _ = queries.shape
    pieces_of = BLK // rows
    width = far[0].shape[3]
    heads = width // HD

    def body(code_ref, q_hbm, *refs):
        far_kernel(frames, near, pieces_of, heads, first_head, code_ref, q_hbm, *refs[:5], *refs[5 + len(after) :])

    result = jax.ShapeDtypeStruct((members, rows, width), jnp.bfloat16)
    return pl.pallas_call(
        body,
        out_shape=[result, jax.ShapeDtypeStruct((8, 128), jnp.float32)],
        in_specs=[pl.BlockSpec(memory_space=pltpu.SMEM)] + [anywhere] * 3 + [in_vmem] * 3 + [anywhere] * len(after),
        out_specs=[in_hbm, in_vmem],
        scratch_shapes=[
            pltpu.VMEM(result.shape, result.dtype),
            *[pltpu.VMEM(array.shape, array.dtype) for array in far],
            pltpu.VMEM(result.shape, result.dtype),
            pltpu.SemaphoreType.DMA((heads, 3)),
            pltpu.SemaphoreType.DMA((heads,)),
        ],
        compiler_params=pltpu.CompilerParams(vmem_limit_bytes=OTHER_VMEM),
        cost_estimate=pl.CostEstimate(**(cost or measured_cost(frames * heads * 4))),
    )(codes, queries, *far, *partials, *after)


def on_device(outer, inner, q_proj, k_proj, v_proj, kv_list):
    frames = inner
    rows, model_width = q_proj.shape
    team = ("inner", "rep", "uly")
    team_size = frames * BPF * BLK // rows
    heads_here = model_width // HD // team_size
    pieces_of = BLK // rows
    per_frame = BPF * pieces_of
    my_group = lax.axis_index("outer")

    def rows_of(reader_frame, count):
        start = jnp.clip(reader_frame * BPF, 0, kv_list.shape[0] - count * BPF)
        return lax.dynamic_slice_in_dim(kv_list, start, count * BPF, 0)

    lists = rows_of(my_group * frames, frames).reshape(frames * BPF, 1, -1)
    first_ids = BPF * (my_group * frames - REACH + lax.broadcasted_iota(jnp.int32, (1, frames + 2 * REACH, 1), 1))
    hits = jnp.where(lists == first_ids, 1, 0) + jnp.where(lists == first_ids + 1, 2, 0)
    codes = jnp.sum(jnp.where(lists >= 0, hits, 0), axis=-1).reshape(-1)

    def picked(reader_frame, holder_frame):
        return jnp.any(rows_of(reader_frame, 1) == holder_frame * BPF + 1).astype(jnp.int32)

    assert sum(CHUNKS) == heads_here
    widths = [heads * HD for heads in CHUNKS]
    lows = [sum(CHUNKS[:c]) for c in range(len(CHUNKS))]
    starts = [low * team_size * HD for low in lows]

    def exchange(array):
        return lax.all_to_all(array, team, split_axis=0, concat_axis=0, tiled=True)

    def shifted(array, heading, hop):
        places = range(outer)
        route = [(i, i + heading) for i in places if i + heading in places and i - (hop - 1) * heading in places]
        return lax.ppermute(array, "outer", route)

    hops = []
    for hop in range(1, -(-REACH // frames) + 1):
        spare = hop * frames - REACH
        hops.append((frames - max(0, spare), spare >= 0))

    def forwarded(held, held_frames, keep, single, after):
        whole = (keep - 1 if single else keep) * per_frame
        if single:
            from_left, from_right = (my_group + 1) * frames, my_group * frames - 1
            edges = held[0].shape[0] - whole - per_frame, whole
            edge_places = jnp.stack(
                [
                    edges[0] + pieces_of * picked(from_left, from_left - REACH),
                    edges[1] + pieces_of * picked(from_right, from_right + REACH),
                ]
            )
            return list(select(held, edge_places, pieces_of, whole, after))
        if keep < held_frames:
            return [held[0][held[0].shape[0] - whole :], held[1][:whole]]
        return held

    def first_hop(own):
        assert hops[0] == (frames, False)
        return [[shifted(own, 1, 1), shifted(own, -1, 1)]]

    def selected(arrivals, after=()):
        for hop in range(1, len(hops)):
            to_send = forwarded(arrivals[-1], hops[hop - 1][0], *hops[hop], after if hop == len(hops) - 1 else ())
            if hop < len(hops) - 1:
                arrivals.append([shifted(to_send[0], 1, hop + 1), shifted(to_send[1], -1, hop + 1)])
        return to_send

    def last_hop(arrivals, to_send):
        arrivals.append([shifted(to_send[0], 1, len(hops)), shifted(to_send[1], -1, len(hops))])

    chunks = range(len(CHUNKS))
    near = (len(hops) - 1) * frames
    packed = [pack([k_proj, v_proj], [starts[c]], [widths[c]], team_size) for c in chunks]
    owned = [exchange(array) for array in packed]
    queries = exchange(pack([q_proj], starts, widths, team_size, after=packed[-1:]))
    arrivals, sent, tokens, outs = [], [], [], []
    partials = {}

    def attend_rest(c, after, cost):
        far = arrivals[c][-1]
        result, token = attend_far(codes, queries, far, partials[c], frames, near, lows[c], cost, after=after)
        tokens.append(token)
        if outs:
            result, outs[-1] = lax.optimization_barrier((result, outs[-1]))
        outs.append(exchange(result))

    for c in chunks:
        arrivals.append(first_hop(owned[c]))
        sent.append(selected(arrivals[c], after=partials[c - 1] if c > 0 else ()))
        order = [a[0] for a in arrivals[c][::-1]] + [owned[c]] + [a[1] for a in arrivals[c]]
        last_hop(arrivals[c], sent[c])
        if c > 0:
            attend_rest(c - 1, sent[c], None)
        after = sent[c] + tokens[-1:]
        cost = little if c == len(CHUNKS) - 1 else None
        partials[c] = list(attend_near(codes, queries, order, frames, near, lows[c], cost, after=after))
    attend_rest(chunks[-1], (), little)
    return unpack(outs, starts, model_width)


def solution(mesh):
    sizes = dict(mesh.shape)
    members = sizes["uly"] * sizes["rep"]
    heads = 40
    inner = max(
        i for i in range(1, sizes["ctx"] + 1) if sizes["ctx"] % i == 0 and heads % (i * members) == 0
    )
    outer = sizes["ctx"] // inner
    finer = Mesh(
        mesh.devices.reshape(sizes["groups"], outer, inner, sizes["uly"], sizes["rep"]),
        ("groups", "outer", "inner", "uly", "rep"),
    )
    split = P(("groups", "outer", "inner", "rep", "uly"), None)
    return jax.shard_map(
        functools.partial(on_device, outer, inner),
        mesh=finer,
        in_specs=(split, split, split, P("groups", None)),
        out_specs=split,
        check_vma=False,
    )
```

profile of v0, /device:TPU:17, one launch (start us, length us, event | category | flops | bytes accessed | tf_op | source)
XLA Modules:
  0.0 151.2 jit_solution(7087779910773061648)
XLA Ops:
  0.0 2.1 %shard_map.48 = bf16[8,2,128,256]{3,2,1,0:T(8,128)(2,1)} custom-call(bf16[128,5120]{1,0:T(8,128)(2,1)} %refs_0_.5, bf16[128,5120]{1,0:T(8,128)(2,1)} %refs_1_.3), custom_call_target="tpu_custom_call" | custom-call | flops 20000000000 | bytes 1024 | tf_op jit(solution)/shard_map/pallas_call | solution.py:99
  2.2 4.8 %all-to-all-start.2 = ((bf16[8,2,128,256]{3,2,1,0:T(8,128)(2,1)}), bf16[8,2,128,256]{3,2,1,0:T(8,128)(2,1)}, u32[]{:S(2)}, u32[]{:S(2)}) async-start(bf16[8,2,128,256]{3,2,1,0:T(8,128)(2,1)} %shard_map.48), calls=%async_computation.2 | async-start | bytes 2097152 | tf_op jit(solution)/shard_map/all_to_all | solution.py:408
  7.0 2.5 %shard_map.46.refs_1_ = bf16[8,2,128,384]{3,2,1,0:T(8,128)(2,1)} custom-call(bf16[128,5120]{1,0:T(8,128)(2,1)} %refs_0_.5, bf16[128,5120]{1,0:T(8,128)(2,1)} %refs_1_.3), custom_call_target="tpu_custom_call" | custom-call | flops 20000000000 | bytes 1024 | tf_op jit(solution)/shard_map/pallas_call | solution.py:99
  12.0 9.1 %all-to-all-done.2.refs_1_ = bf16[8,2,128,256]{3,2,1,0:T(8,128)(2,1)} async-done(((bf16[8,2,128,256]{3,2,1,0:T(8,128)(2,1)}), bf16[8,2,128,256]{3,2,1,0:T(8,128)(2,1)}, u32[]{:S(2)}, u32[]{:S(2)}) %all-to-all-start.2) | async-done | bytes 1048608 | tf_op jit(solution)/shard_map/all_to_all | solution.py:408
  21.2 4.3 %all-to-all-start.1 = ((bf16[8,2,128,384]{3,2,1,0:T(8,128)(2,1)}), bf16[8,2,128,384]{3,2,1,0:T(8,128)(2,1)S(1)}, u32[]{:S(2)}, u32[]{:S(2)}) async-start(bf16[8,2,128,384]{3,2,1,0:T(8,128)(2,1)} %shard_map.46.refs_1_), calls=%async_computation.1 | async-start | bytes 3145728 | tf_op jit(solution)/shard_map/all_to_all | solution.py:408
  27.6 4.2 %collective-permute-start.2 = (bf16[8,2,128,256]{3,2,1,0:T(8,128)(2,1)}, bf16[8,2,128,256]{3,2,1,0:T(8,128)(2,1)}, u32[]{:S(2)}, u32[]{:S(2)}) collective-permute-start(bf16[8,2,128,256]{3,2,1,0:T(8,128)(2,1)} %all-to-all-done.2.refs_1_), channel_id=1, source_target_pairs={{0,8},{8,16},{16,24},{1,9},{9,17},{17,25},{2,10},{10,18},{18,26},{... | collective-permute-start | bytes 3145736 | tf_op jit(solution)/shard_map/ppermute | solution.py:413
  31.8 2.3 %shard_map.47 = bf16[8,1,128,640]{3,2,1,0:T(8,128)(2,1)} custom-call(bf16[128,5120]{1,0:T(8,128)(2,1)} %refs_0_.4, bf16[8,2,128,384]{3,2,1,0:T(8,128)(2,1)} %shard_map.46.refs_1_), custom_call_target="tpu_custom_call" | custom-call | flops 20000000000 | bytes 1024 | tf_op jit(solution)/shard_map/pallas_call | solution.py:99
  34.2 11.2 %all-to-all-done.1.refs_1_ = bf16[8,2,128,384]{3,2,1,0:T(8,128)(2,1)S(1)} async-done(((bf16[8,2,128,384]{3,2,1,0:T(8,128)(2,1)}), bf16[8,2,128,384]{3,2,1,0:T(8,128)(2,1)S(1)}, u32[]{:S(2)}, u32[]{:S(2)}) %all-to-all-start.1) | async-done | bytes 1572896 | tf_op jit(solution)/shard_map/all_to_all | solution.py:408
  45.4 4.2 %all-to-all-start = ((bf16[8,1,128,640]{3,2,1,0:T(8,128)(2,1)}), bf16[8,1,128,640]{3,2,1,0:T(8,128)(2,1)S(1)}, u32[]{:S(2)}, u32[]{:S(2)}) async-start(bf16[8,1,128,640]{3,2,1,0:T(8,128)(2,1)} %shard_map.47), calls=%async_computation | async-start | bytes 2621440 | tf_op jit(solution)/shard_map/all_to_all | solution.py:408
  51.7 4.3 %collective-permute-start = (bf16[8,2,128,384]{3,2,1,0:T(8,128)(2,1)S(1)}, bf16[8,2,128,384]{3,2,1,0:T(8,128)(2,1)}, u32[]{:S(2)}, u32[]{:S(2)}) collective-permute-start(bf16[8,2,128,384]{3,2,1,0:T(8,128)(2,1)S(1)} %all-to-all-done.1.refs_1_), channel_id=1, source_target_pairs={{0,8},{8,16},{16,24},{1,9},{9,17},{17,25},{2,10},{10,18},{18,26},{... | collective-permute-start | bytes 4718600 | tf_op jit(solution)/shard_map/ppermute | solution.py:413
  56.0 2.7 %shard_map.49 = (bf16[5,2,128,256]{3,2,1,0:T(8,128)(2,1)}, bf16[5,2,128,256]{3,2,1,0:T(8,128)(2,1)}) custom-call(s32[2]{0:T(128)S(1)} %pad_add_fusion.refs_0_, bf16[8,2,128,256]{3,2,1,0:T(8,128)(2,1)} %collective-permute-done.2.refs_1_.refs_0_, bf16[8,2,128,256]{3,2,1,0:T(8,128)(2,1)} %collective-permute-done.3.refs_2_), custom_call_target="tpu_custom_call" | custom-call | flops 99999997952 | bytes 1024 | tf_op jit(solution)/shard_map/pallas_call | solution.py:53
  58.8 2.4 %collective-permute-start.6 = (bf16[5,2,128,256]{3,2,1,0:T(8,128)(2,1)}, bf16[5,2,128,256]{3,2,1,0:T(8,128)(2,1)}, u32[]{:S(2)}, u32[]{:S(2)}) collective-permute-start(bf16[5,2,128,256]{3,2,1,0:T(8,128)(2,1)} %get-tuple-element.20.refs_3_), channel_id=1, source_target_pairs={{8,16},{16,24},{9,17},{17,25},{10,18},{18,26},{11,19},{19,27},{12,... | collective-permute-start | bytes 1966088 | tf_op jit(solution)/shard_map/ppermute | solution.py:413
  61.2 4.7 %collective-permute-start.7 = (bf16[5,2,128,256]{3,2,1,0:T(8,128)(2,1)}, bf16[5,2,128,256]{3,2,1,0:T(8,128)(2,1)}, u32[]{:S(2)}, u32[]{:S(2)}) collective-permute-start(bf16[5,2,128,256]{3,2,1,0:T(8,128)(2,1)} %get-tuple-element.21.refs_4_), channel_id=1, source_target_pairs={{8,0},{16,8},{9,1},{17,9},{10,2},{18,10},{11,3},{19,11},{12,4},{20... | collective-permute-start | bytes 1966088 | tf_op jit(solution)/shard_map/ppermute | solution.py:413
  66.6 8.9 %shard_map.50 = (f32[2,4,256,128]{3,2,1,0:T(8,128)S(1)}, f32[2,4,256,128]{3,2,1,0:T(8,128)S(1)}, f32[2,4,256,128]{3,2,1,0:T(8,128)S(1)}) custom-call(s32[144]{0:T(256)S(1)} %reshape.17.code_ref, bf16[8,1,128,640]{3,2,1,0:T(8,128)(2,1)S(1)} %all-to-all-done.q_hbm, bf16[8,2,128,256]{3,2,1,0:T(8,128)(2,1)} %collective-permute-done.2.refs_1_.refs_0_, ...), custom_call_target="tpu_custom_call" | custom-call | flops 10468982784 | bytes 1024 | tf_op jit(solution)/shard_map/pallas_call | solution.py:338
  75.5 12.1 %collective-permute-done.1.refs_2_ = bf16[8,2,128,384]{3,2,1,0:T(8,128)(2,1)} collective-permute-done((bf16[8,2,128,384]{3,2,1,0:T(8,128)(2,1)S(1)}, bf16[8,2,128,384]{3,2,1,0:T(8,128)(2,1)}, u32[]{:S(2)}, u32[]{:S(2)}) %collective-permute-start.1) | collective-permute-done | bytes 1572896 | tf_op jit(solution)/shard_map/ppermute | solution.py:413
  89.4 3.1 %shard_map.51 = (bf16[5,2,128,384]{3,2,1,0:T(8,128)(2,1)}, bf16[5,2,128,384]{3,2,1,0:T(8,128)(2,1)}) custom-call(s32[2]{0:T(128)S(1)} %pad_add_fusion.refs_0_, bf16[8,2,128,384]{3,2,1,0:T(8,128)(2,1)} %collective-permute-done.refs_1_.refs_0_, bf16[8,2,128,384]{3,2,1,0:T(8,128)(2,1)} %collective-permute-done.1.refs_2_, ...), custom_call_target="tpu_custom_call" | custom-call | flops 99999997952 | bytes 1024 | tf_op jit(solution)/shard_map/pallas_call | solution.py:53
  92.5 4.2 %collective-permute-start.4 = (bf16[5,2,128,384]{3,2,1,0:T(8,128)(2,1)}, bf16[5,2,128,384]{3,2,1,0:T(8,128)(2,1)}, u32[]{:S(2)}, u32[]{:S(2)}) collective-permute-start(bf16[5,2,128,384]{3,2,1,0:T(8,128)(2,1)} %get-tuple-element.25.refs_5_.refs_3_), channel_id=1, source_target_pairs={{8,16},{16,24},{9,17},{17,25},{10,18},{18,26},{11,19},{19,27},{12,... | collective-permute-start | bytes 2949128 | tf_op jit(solution)/shard_map/ppermute | solution.py:413
  96.7 3.0 %collective-permute-start.5 = (bf16[5,2,128,384]{3,2,1,0:T(8,128)(2,1)}, bf16[5,2,128,384]{3,2,1,0:T(8,128)(2,1)}, u32[]{:S(2)}, u32[]{:S(2)}) collective-permute-start(bf16[5,2,128,384]{3,2,1,0:T(8,128)(2,1)} %get-tuple-element.26.refs_6_.refs_4_), channel_id=1, source_target_pairs={{8,0},{16,8},{9,1},{17,9},{10,2},{18,10},{11,3},{19,11},{12,4},{20... | collective-permute-start | bytes 2949128 | tf_op jit(solution)/shard_map/ppermute | solution.py:413
  99.7 3.9 %collective-permute-done.6.refs_0_ = bf16[5,2,128,256]{3,2,1,0:T(8,128)(2,1)} collective-permute-done((bf16[5,2,128,256]{3,2,1,0:T(8,128)(2,1)}, bf16[5,2,128,256]{3,2,1,0:T(8,128)(2,1)}, u32[]{:S(2)}, u32[]{:S(2)}) %collective-permute-start.6) | collective-permute-done | bytes 655392 | tf_op jit(solution)/shard_map/ppermute | solution.py:413
  103.6 4.7 %shard_map.52 = (bf16[8,128,256]{2,1,0:T(8,128)(2,1)S(1)}, f32[8,128]{1,0:T(8,128)S(1)}) custom-call(s32[144]{0:T(256)S(1)} %reshape.17.code_ref, bf16[8,1,128,640]{3,2,1,0:T(8,128)(2,1)S(1)} %all-to-all-done.q_hbm, bf16[5,2,128,256]{3,2,1,0:T(8,128)(2,1)} %collective-permute-done.6.refs_0_, bf16[5,2,128,256]{3,2,1,0:T(8,128)(2,1)} %collective-permute-done.7.refs_1_, ...), custom_call_target="tpu_custom_call" | custom-call | flops 3221225472 | bytes 1024 | tf_op jit(solution)/shard_map/pallas_call | solution.py:363
  109.1 6.1 %all-to-all-start.3 = ((bf16[8,128,256]{2,1,0:T(8,128)(2,1)}), bf16[8,128,256]{2,1,0:T(8,128)(2,1)S(1)}, u32[]{:S(2)}, u32[]{:S(2)}) async-start(bf16[8,128,256]{2,1,0:T(8,128)(2,1)} %copy-done), calls=%async_computation.3 | async-start | bytes 1048576 | tf_op jit(solution)/shard_map/all_to_all | solution.py:408
  115.2 12.4 %shard_map.53 = (f32[3,4,256,128]{3,2,1,0:T(8,128)S(1)}, f32[3,4,256,128]{3,2,1,0:T(8,128)S(1)}, f32[3,4,256,128]{3,2,1,0:T(8,128)S(1)}) custom-call(s32[144]{0:T(256)S(1)} %reshape.17.code_ref, bf16[8,1,128,640]{3,2,1,0:T(8,128)(2,1)S(1)} %all-to-all-done.q_hbm, bf16[8,2,128,384]{3,2,1,0:T(8,128)(2,1)} %collective-permute-done.refs_1_.refs_0_, ...), custom_call_target="tpu_custom_call" | custom-call | flops 1024 | bytes 1024 | tf_op jit(solution)/shard_map/pallas_call | solution.py:338
  127.6 6.8 %shard_map.54 = (bf16[8,128,384]{2,1,0:T(8,128)(2,1)S(1)}, f32[8,128]{1,0:T(8,128)}) custom-call(s32[144]{0:T(256)S(1)} %reshape.17.code_ref, bf16[8,1,128,640]{3,2,1,0:T(8,128)(2,1)S(1)} %all-to-all-done.q_hbm, bf16[5,2,128,384]{3,2,1,0:T(8,128)(2,1)} %collective-permute-done.4.refs_0_, bf16[5,2,128,384]{3,2,1,0:T(8,128)(2,1)} %collective-permute-done.5.refs_1_, ...), custom_call_target="tpu_custom_call" | custom-call | flops 1024 | bytes 1024 | tf_op jit(solution)/shard_map/pallas_call | solution.py:363
  134.4 15.7 %all_to_all.25.refs_1_ = bf16[8,128,384]{2,1,0:T(8,128)(2,1)S(1)} all-to-all(bf16[8,128,384]{2,1,0:T(8,128)(2,1)S(1)} %get-tuple-element.34), channel_id=1, replica_groups=mesh['groups'=1,'outer'=4,'inner'=4,'uly'=2,'rep'=1] {'inner','rep','uly'}, dimensions={0} | all-to-all | bytes 1572864 | tf_op jit(solution)/shard_map/all_to_all | solution.py:408
  (23 shorter events, 10.0 us)
Async XLA Ops:
  2.2 19.0 %all-to-all-start.2 = ((bf16[8,2,128,256]{3,2,1,0:T(8,128)(2,1)}), bf16[8,2,128,256]{3,2,1,0:T(8,128)(2,1)}, u32[]{:S(2)}, u32[]{:S(2)}) async-start(bf16[8,2,128,256]{3,2,1,0:T(8,128)(2,1)} %shard_map.48), calls=%async_computation.2 | async-start | bytes 2097152 | tf_op jit(solution)/shard_map/all_to_all | solution.py:408
  7.0 2.5 %copy-start.1 = (s32[32,16]{0,1:T(8,128)S(1)}, s32[32,16]{0,1:T(8,128)}, u32[]{:S(2)}) copy-start(s32[32,16]{0,1:T(8,128)} %param.7) | copy-start | bytes 6148
  21.2 24.2 %all-to-all-start.1 = ((bf16[8,2,128,384]{3,2,1,0:T(8,128)(2,1)}), bf16[8,2,128,384]{3,2,1,0:T(8,128)(2,1)S(1)}, u32[]{:S(2)}, u32[]{:S(2)}) async-start(bf16[8,2,128,384]{3,2,1,0:T(8,128)(2,1)} %shard_map.46.refs_1_), calls=%async_computation.1 | async-start | bytes 3145728 | tf_op jit(solution)/shard_map/all_to_all | solution.py:408
  25.5 30.5 %collective-permute-start.3 = (bf16[8,2,128,256]{3,2,1,0:T(8,128)(2,1)}, bf16[8,2,128,256]{3,2,1,0:T(8,128)(2,1)}, u32[]{:S(2)}, u32[]{:S(2)}) collective-permute-start(bf16[8,2,128,256]{3,2,1,0:T(8,128)(2,1)} %all-to-all-done.2.refs_1_), channel_id=1, source_target_pairs={{8,0},{16,8},{24,16},{9,1},{17,9},{25,17},{10,2},{18,10},{26,18},{... | collective-permute-start | bytes 3145736 | tf_op jit(solution)/shard_map/ppermute | solution.py:413
  27.6 28.4 %collective-permute-start.2 = (bf16[8,2,128,256]{3,2,1,0:T(8,128)(2,1)}, bf16[8,2,128,256]{3,2,1,0:T(8,128)(2,1)}, u32[]{:S(2)}, u32[]{:S(2)}) collective-permute-start(bf16[8,2,128,256]{3,2,1,0:T(8,128)(2,1)} %all-to-all-done.2.refs_1_), channel_id=1, source_target_pairs={{0,8},{8,16},{16,24},{1,9},{9,17},{17,25},{2,10},{10,18},{18,26},{... | collective-permute-start | bytes 3145736 | tf_op jit(solution)/shard_map/ppermute | solution.py:413
  45.4 21.2 %all-to-all-start = ((bf16[8,1,128,640]{3,2,1,0:T(8,128)(2,1)}), bf16[8,1,128,640]{3,2,1,0:T(8,128)(2,1)S(1)}, u32[]{:S(2)}, u32[]{:S(2)}) async-start(bf16[8,1,128,640]{3,2,1,0:T(8,128)(2,1)} %shard_map.47), calls=%async_computation | async-start | bytes 2621440 | tf_op jit(solution)/shard_map/all_to_all | solution.py:408
  49.6 38.0 %collective-permute-start.1 = (bf16[8,2,128,384]{3,2,1,0:T(8,128)(2,1)S(1)}, bf16[8,2,128,384]{3,2,1,0:T(8,128)(2,1)}, u32[]{:S(2)}, u32[]{:S(2)}) collective-permute-start(bf16[8,2,128,384]{3,2,1,0:T(8,128)(2,1)S(1)} %all-to-all-done.1.refs_1_), channel_id=1, source_target_pairs={{8,0},{16,8},{24,16},{9,1},{17,9},{25,17},{10,2},{18,10},{26,18},{... | collective-permute-start | bytes 4718600 | tf_op jit(solution)/shard_map/ppermute | solution.py:413
  51.7 37.7 %collective-permute-start = (bf16[8,2,128,384]{3,2,1,0:T(8,128)(2,1)S(1)}, bf16[8,2,128,384]{3,2,1,0:T(8,128)(2,1)}, u32[]{:S(2)}, u32[]{:S(2)}) collective-permute-start(bf16[8,2,128,384]{3,2,1,0:T(8,128)(2,1)S(1)} %all-to-all-done.1.refs_1_), channel_id=1, source_target_pairs={{0,8},{8,16},{16,24},{1,9},{9,17},{17,25},{2,10},{10,18},{18,26},{... | collective-permute-start | bytes 4718600 | tf_op jit(solution)/shard_map/ppermute | solution.py:413
  58.8 44.8 %collective-permute-start.6 = (bf16[5,2,128,256]{3,2,1,0:T(8,128)(2,1)}, bf16[5,2,128,256]{3,2,1,0:T(8,128)(2,1)}, u32[]{:S(2)}, u32[]{:S(2)}) collective-permute-start(bf16[5,2,128,256]{3,2,1,0:T(8,128)(2,1)} %get-tuple-element.20.refs_3_), channel_id=1, source_target_pairs={{8,16},{16,24},{9,17},{17,25},{10,18},{18,26},{11,19},{19,27},{12,... | collective-permute-start | bytes 1966088 | tf_op jit(solution)/shard_map/ppermute | solution.py:413
  61.2 42.4 %collective-permute-start.7 = (bf16[5,2,128,256]{3,2,1,0:T(8,128)(2,1)}, bf16[5,2,128,256]{3,2,1,0:T(8,128)(2,1)}, u32[]{:S(2)}, u32[]{:S(2)}) collective-permute-start(bf16[5,2,128,256]{3,2,1,0:T(8,128)(2,1)} %get-tuple-element.21.refs_4_), channel_id=1, source_target_pairs={{8,0},{16,8},{9,1},{17,9},{10,2},{18,10},{11,3},{19,11},{12,4},{20... | collective-permute-start | bytes 1966088 | tf_op jit(solution)/shard_map/ppermute | solution.py:413
  92.5 35.1 %collective-permute-start.4 = (bf16[5,2,128,384]{3,2,1,0:T(8,128)(2,1)}, bf16[5,2,128,384]{3,2,1,0:T(8,128)(2,1)}, u32[]{:S(2)}, u32[]{:S(2)}) collective-permute-start(bf16[5,2,128,384]{3,2,1,0:T(8,128)(2,1)} %get-tuple-element.25.refs_5_.refs_3_), channel_id=1, source_target_pairs={{8,16},{16,24},{9,17},{17,25},{10,18},{18,26},{11,19},{19,27},{12,... | collective-permute-start | bytes 2949128 | tf_op jit(solution)/shard_map/ppermute | solution.py:413
  96.7 30.8 %collective-permute-start.5 = (bf16[5,2,128,384]{3,2,1,0:T(8,128)(2,1)}, bf16[5,2,128,384]{3,2,1,0:T(8,128)(2,1)}, u32[]{:S(2)}, u32[]{:S(2)}) collective-permute-start(bf16[5,2,128,384]{3,2,1,0:T(8,128)(2,1)} %get-tuple-element.26.refs_6_.refs_4_), channel_id=1, source_target_pairs={{8,0},{16,8},{9,1},{17,9},{10,2},{18,10},{11,3},{19,11},{12,4},{20... | collective-permute-start | bytes 2949128 | tf_op jit(solution)/shard_map/ppermute | solution.py:413
  108.3 0.8 copy-start
  109.1 25.3 %all-to-all-start.3 = ((bf16[8,128,256]{2,1,0:T(8,128)(2,1)}), bf16[8,128,256]{2,1,0:T(8,128)(2,1)S(1)}, u32[]{:S(2)}, u32[]{:S(2)}) async-start(bf16[8,128,256]{2,1,0:T(8,128)(2,1)} %copy-done), calls=%async_computation.3 | async-start | bytes 1048576 | tf_op jit(solution)/shard_map/all_to_all | solution.py:408
where the time goes:
time: 153 us; the launch traced here: 151 us
  Pallas kernels  46.7 us (31%)
  starting transfers between devices  46.5 us (30%)
  waiting for transfers between devices  38.9 us (25%)
  blocking collectives  15.7 us (10%)
  between operations  1.53 us (1%)
    ppermute x8, starting transfers between devices, shifted(): return lax.ppermute(array, 'outer', route)  27 us
    pallas_call x2, Pallas kernels, attend_near(): pl.pallas_call(body, out_shape=[partial] * 3, in_specs=[pl.BlockSpec(memo...  21.2 us
    all_to_all x4, waiting for transfers between devices, exchange(): return lax.all_to_all(array, team, split_axis=0, concat_axis=0, tiled=True)  21.1 us
    all_to_all x4, starting transfers between devices, exchange(): return lax.all_to_all(array, team, split_axis=0, concat_axis=0, tiled=True)  19.5 us
    ppermute x8, waiting for transfers between devices, shifted(): return lax.ppermute(array, 'outer', route)  17.8 us
    all_to_all x1, blocking collectives, exchange(): return lax.all_to_all(array, team, split_axis=0, concat_axis=0, tiled=True)  15.7 us
    pallas_call x2, Pallas kernels, attend_far(): pl.pallas_call(body, out_shape=[result, jax.ShapeDtypeStruct((8, 128), jn...  11.5 us
    pallas_call x3, Pallas kernels, pack(): pl.pallas_call(body, out_shape=jax.ShapeDtypeStruct((team_size, len(array...  6.96 us
  transfers between devices with their start and end apart: 12, of which 6 were waited for; matrix products, arithmetic and copies ran while one was open for 1% of the time, Pallas kernels for 29%

commit v1 on v0

--- a/solution.py
+++ b/solution.py
@@ -144,14 +144,14 @@
         for side, (source, stage, out) in enumerate(zip(sources, stages, outs)):
             one = pl.ds(0 if side == 0 else whole, count)
             steps.append((source.at[pl.ds(place_ref[side], count)], stage.at[one], out.at[one]))
-            if whole > 0:
-                rest = pl.ds(count if side == 0 else 0, whole)
-                kept = pl.ds(source.shape[0] - whole if side == 0 else 0, whole)
+            for low in range(0, whole, count):
+                rest = pl.ds(low + (count if side == 0 else 0), count)
+                kept = pl.ds(low + (source.shape[0] - whole if side == 0 else 0), count)
                 steps.append((source.at[kept], stage.at[rest], out.at[rest]))
         return steps
 
     shapes = [jax.ShapeDtypeStruct((count + whole,) + array.shape[1:], array.dtype) for array in held]
-    return copy_call(plan, shapes, 2 * (2 if whole > 0 else 1), held, scalars=[places], after=after, cost=much)
+    return copy_call(plan, shapes, 2 * (1 + whole // count), held, scalars=[places], after=after, cost=much)
 
 
 def columns_of(head):
@@ -253,7 +253,7 @@
         top_ref[head, frame] = jnp.broadcast_to(jnp.concatenate(tops, axis=0), mixed.shape)
         total_ref[head, frame] = jnp.broadcast_to(totals, mixed.shape)
 
-    together = 2 if frames % 2 == 0 else 1
+    together = math.gcd(frames, 4)
 
     def work(head):
         def step(index, carry):

time: 153 us -> 152 us (level)
  transfers between devices with their start and end apart: 12 -> 12, of which waited for: 6 -> 6; matrix products, arithmetic and copies ran while one was open for 1% -> 1% of each run, Pallas kernels for 29% -> 28%
where the time goes in v1:
time: 152 us; the launch traced here: 151 us
  starting transfers between devices  46.5 us (31%)
  Pallas kernels  45.5 us (30%)
  waiting for transfers between devices  39.4 us (26%)
  blocking collectives  15.7 us (10%)
  between operations  1.53 us (1%)
    ppermute x8, starting transfers between devices, shifted(): return lax.ppermute(array, 'outer', route)  27 us
    all_to_all x4, waiting for transfers between devices, exchange(): return lax.all_to_all(array, team, split_axis=0, concat_axis=0, tiled=True)  21.1 us
    pallas_call x2, Pallas kernels, attend_near(): pl.pallas_call(body, out_shape=[partial] * 3, in_specs=[pl.BlockSpec(memo...  20.1 us
    all_to_all x4, starting transfers between devices, exchange(): return lax.all_to_all(array, team, split_axis=0, concat_axis=0, tiled=True)  19.5 us
    ppermute x8, waiting for transfers between devices, shifted(): return lax.ppermute(array, 'outer', route)  18.3 us
    all_to_all x1, blocking collectives, exchange(): return lax.all_to_all(array, team, split_axis=0, concat_axis=0, tiled=True)  15.7 us
    pallas_call x2, Pallas kernels, attend_far(): pl.pallas_call(body, out_shape=[result, jax.ShapeDtypeStruct((8, 128), jn...  11.5 us
    pallas_call x3, Pallas kernels, pack(): pl.pallas_call(body, out_shape=jax.ShapeDtypeStruct((team_size, len(array...  6.96 us
  transfers between devices with their start and end apart: 12, of which 6 were waited for; matrix products, arithmetic and copies ran while one was open for 1% of the time, Pallas kernels for 28%

profile of v1, /device:TPU:17, one launch (start us, length us, event | category | flops | bytes accessed | tf_op | source)
XLA Modules:
  0.0 150.6 jit_solution(16664932792377490032)
XLA Ops:
  0.0 2.1 %shard_map.48 = bf16[8,2,128,256]{3,2,1,0:T(8,128)(2,1)} custom-call(bf16[128,5120]{1,0:T(8,128)(2,1)} %refs_0_.5, bf16[128,5120]{1,0:T(8,128)(2,1)} %refs_1_.3), custom_call_target="tpu_custom_call" | custom-call | flops 20000000000 | bytes 1024 | tf_op jit(solution)/shard_map/pallas_call | solution.py:99
  2.2 4.8 %all-to-all-start.2 = ((bf16[8,2,128,256]{3,2,1,0:T(8,128)(2,1)}), bf16[8,2,128,256]{3,2,1,0:T(8,128)(2,1)}, u32[]{:S(2)}, u32[]{:S(2)}) async-start(bf16[8,2,128,256]{3,2,1,0:T(8,128)(2,1)} %shard_map.48), calls=%async_computation.2 | async-start | bytes 2097152 | tf_op jit(solution)/shard_map/all_to_all | solution.py:408
  7.0 2.5 %shard_map.46.refs_1_ = bf16[8,2,128,384]{3,2,1,0:T(8,128)(2,1)} custom-call(bf16[128,5120]{1,0:T(8,128)(2,1)} %refs_0_.5, bf16[128,5120]{1,0:T(8,128)(2,1)} %refs_1_.3), custom_call_target="tpu_custom_call" | custom-call | flops 20000000000 | bytes 1024 | tf_op jit(solution)/shard_map/pallas_call | solution.py:99
  12.0 9.1 %all-to-all-done.2.refs_1_ = bf16[8,2,128,256]{3,2,1,0:T(8,128)(2,1)} async-done(((bf16[8,2,128,256]{3,2,1,0:T(8,128)(2,1)}), bf16[8,2,128,256]{3,2,1,0:T(8,128)(2,1)}, u32[]{:S(2)}, u32[]{:S(2)}) %all-to-all-start.2) | async-done | bytes 1048608 | tf_op jit(solution)/shard_map/all_to_all | solution.py:408
  21.2 4.3 %all-to-all-start.1 = ((bf16[8,2,128,384]{3,2,1,0:T(8,128)(2,1)}), bf16[8,2,128,384]{3,2,1,0:T(8,128)(2,1)S(1)}, u32[]{:S(2)}, u32[]{:S(2)}) async-start(bf16[8,2,128,384]{3,2,1,0:T(8,128)(2,1)} %shard_map.46.refs_1_), calls=%async_computation.1 | async-start | bytes 3145728 | tf_op jit(solution)/shard_map/all_to_all | solution.py:408
  27.6 4.2 %collective-permute-start.2 = (bf16[8,2,128,256]{3,2,1,0:T(8,128)(2,1)}, bf16[8,2,128,256]{3,2,1,0:T(8,128)(2,1)}, u32[]{:S(2)}, u32[]{:S(2)}) collective-permute-start(bf16[8,2,128,256]{3,2,1,0:T(8,128)(2,1)} %all-to-all-done.2.refs_1_), channel_id=1, source_target_pairs={{0,8},{8,16},{16,24},{1,9},{9,17},{17,25},{2,10},{10,18},{18,26},{... | collective-permute-start | bytes 3145736 | tf_op jit(solution)/shard_map/ppermute | solution.py:413
  31.8 2.3 %shard_map.47 = bf16[8,1,128,640]{3,2,1,0:T(8,128)(2,1)} custom-call(bf16[128,5120]{1,0:T(8,128)(2,1)} %refs_0_.4, bf16[8,2,128,384]{3,2,1,0:T(8,128)(2,1)} %shard_map.46.refs_1_), custom_call_target="tpu_custom_call" | custom-call | flops 20000000000 | bytes 1024 | tf_op jit(solution)/shard_map/pallas_call | solution.py:99
  34.2 11.2 %all-to-all-done.1.refs_1_ = bf16[8,2,128,384]{3,2,1,0:T(8,128)(2,1)S(1)} async-done(((bf16[8,2,128,384]{3,2,1,0:T(8,128)(2,1)}), bf16[8,2,128,384]{3,2,1,0:T(8,128)(2,1)S(1)}, u32[]{:S(2)}, u32[]{:S(2)}) %all-to-all-start.1) | async-done | bytes 1572896 | tf_op jit(solution)/shard_map/all_to_all | solution.py:408
  45.4 4.2 %all-to-all-start = ((bf16[8,1,128,640]{3,2,1,0:T(8,128)(2,1)}), bf16[8,1,128,640]{3,2,1,0:T(8,128)(2,1)S(1)}, u32[]{:S(2)}, u32[]{:S(2)}) async-start(bf16[8,1,128,640]{3,2,1,0:T(8,128)(2,1)} %shard_map.47), calls=%async_computation | async-start | bytes 2621440 | tf_op jit(solution)/shard_map/all_to_all | solution.py:408
  51.7 4.3 %collective-permute-start = (bf16[8,2,128,384]{3,2,1,0:T(8,128)(2,1)S(1)}, bf16[8,2,128,384]{3,2,1,0:T(8,128)(2,1)}, u32[]{:S(2)}, u32[]{:S(2)}) collective-permute-start(bf16[8,2,128,384]{3,2,1,0:T(8,128)(2,1)S(1)} %all-to-all-done.1.refs_1_), channel_id=1, source_target_pairs={{0,8},{8,16},{16,24},{1,9},{9,17},{17,25},{2,10},{10,18},{18,26},{... | collective-permute-start | bytes 4718600 | tf_op jit(solution)/shard_map/ppermute | solution.py:413
  56.0 2.8 %shard_map.49 = (bf16[5,2,128,256]{3,2,1,0:T(8,128)(2,1)}, bf16[5,2,128,256]{3,2,1,0:T(8,128)(2,1)}) custom-call(s32[2]{0:T(128)S(1)} %pad_add_fusion.refs_0_, bf16[8,2,128,256]{3,2,1,0:T(8,128)(2,1)} %collective-permute-done.2.refs_1_.refs_0_, bf16[8,2,128,256]{3,2,1,0:T(8,128)(2,1)} %collective-permute-done.3.refs_2_), custom_call_target="tpu_custom_call" | custom-call | flops 99999997952 | bytes 1024 | tf_op jit(solution)/shard_map/pallas_call | solution.py:53
  58.8 2.4 %collective-permute-start.6 = (bf16[5,2,128,256]{3,2,1,0:T(8,128)(2,1)}, bf16[5,2,128,256]{3,2,1,0:T(8,128)(2,1)}, u32[]{:S(2)}, u32[]{:S(2)}) collective-permute-start(bf16[5,2,128,256]{3,2,1,0:T(8,128)(2,1)} %get-tuple-element.20.refs_3_), channel_id=1, source_target_pairs={{8,16},{16,24},{9,17},{17,25},{10,18},{18,26},{11,19},{19,27},{12,... | collective-permute-start | bytes 1966088 | tf_op jit(solution)/shard_map/ppermute | solution.py:413
  61.2 4.7 %collective-permute-start.7 = (bf16[5,2,128,256]{3,2,1,0:T(8,128)(2,1)}, bf16[5,2,128,256]{3,2,1,0:T(8,128)(2,1)}, u32[]{:S(2)}, u32[]{:S(2)}) collective-permute-start(bf16[5,2,128,256]{3,2,1,0:T(8,128)(2,1)} %get-tuple-element.21.refs_4_), channel_id=1, source_target_pairs={{8,0},{16,8},{9,1},{17,9},{10,2},{18,10},{11,3},{19,11},{12,4},{20... | collective-permute-start | bytes 1966088 | tf_op jit(solution)/shard_map/ppermute | solution.py:413
  66.6 8.5 %shard_map.50 = (f32[2,4,256,128]{3,2,1,0:T(8,128)S(1)}, f32[2,4,256,128]{3,2,1,0:T(8,128)S(1)}, f32[2,4,256,128]{3,2,1,0:T(8,128)S(1)}) custom-call(s32[144]{0:T(256)S(1)} %reshape.17.code_ref, bf16[8,1,128,640]{3,2,1,0:T(8,128)(2,1)S(1)} %all-to-all-done.q_hbm, bf16[8,2,128,256]{3,2,1,0:T(8,128)(2,1)} %collective-permute-done.2.refs_1_.refs_0_, ...), custom_call_target="tpu_custom_call" | custom-call | flops 10468982784 | bytes 1024 | tf_op jit(solution)/shard_map/pallas_call | solution.py:338
  75.1 12.5 %collective-permute-done.1.refs_2_ = bf16[8,2,128,384]{3,2,1,0:T(8,128)(2,1)} collective-permute-done((bf16[8,2,128,384]{3,2,1,0:T(8,128)(2,1)S(1)}, bf16[8,2,128,384]{3,2,1,0:T(8,128)(2,1)}, u32[]{:S(2)}, u32[]{:S(2)}) %collective-permute-start.1) | collective-permute-done | bytes 1572896 | tf_op jit(solution)/shard_map/ppermute | solution.py:413
  89.4 3.0 %shard_map.51 = (bf16[5,2,128,384]{3,2,1,0:T(8,128)(2,1)}, bf16[5,2,128,384]{3,2,1,0:T(8,128)(2,1)}) custom-call(s32[2]{0:T(128)S(1)} %pad_add_fusion.refs_0_, bf16[8,2,128,384]{3,2,1,0:T(8,128)(2,1)} %collective-permute-done.refs_1_.refs_0_, bf16[8,2,128,384]{3,2,1,0:T(8,128)(2,1)} %collective-permute-done.1.refs_2_, ...), custom_call_target="tpu_custom_call" | custom-call | flops 99999997952 | bytes 1024 | tf_op jit(solution)/shard_map/pallas_call | solution.py:53
  92.4 4.2 %collective-permute-start.4 = (bf16[5,2,128,384]{3,2,1,0:T(8,128)(2,1)}, bf16[5,2,128,384]{3,2,1,0:T(8,128)(2,1)}, u32[]{:S(2)}, u32[]{:S(2)}) collective-permute-start(bf16[5,2,128,384]{3,2,1,0:T(8,128)(2,1)} %get-tuple-element.25.refs_5_.refs_3_), channel_id=1, source_target_pairs={{8,16},{16,24},{9,17},{17,25},{10,18},{18,26},{11,19},{19,27},{12,... | collective-permute-start | bytes 2949128 | tf_op jit(solution)/shard_map/ppermute | solution.py:413
  96.6 3.0 %collective-permute-start.5 = (bf16[5,2,128,384]{3,2,1,0:T(8,128)(2,1)}, bf16[5,2,128,384]{3,2,1,0:T(8,128)(2,1)}, u32[]{:S(2)}, u32[]{:S(2)}) collective-permute-start(bf16[5,2,128,384]{3,2,1,0:T(8,128)(2,1)} %get-tuple-element.26.refs_6_.refs_4_), channel_id=1, source_target_pairs={{8,0},{16,8},{9,1},{17,9},{10,2},{18,10},{11,3},{19,11},{12,4},{20... | collective-permute-start | bytes 2949128 | tf_op jit(solution)/shard_map/ppermute | solution.py:413
  99.6 3.9 %collective-permute-done.6.refs_0_ = bf16[5,2,128,256]{3,2,1,0:T(8,128)(2,1)} collective-permute-done((bf16[5,2,128,256]{3,2,1,0:T(8,128)(2,1)}, bf16[5,2,128,256]{3,2,1,0:T(8,128)(2,1)}, u32[]{:S(2)}, u32[]{:S(2)}) %collective-permute-start.6) | collective-permute-done | bytes 655392 | tf_op jit(solution)/shard_map/ppermute | solution.py:413
  103.6 4.7 %shard_map.52 = (bf16[8,128,256]{2,1,0:T(8,128)(2,1)S(1)}, f32[8,128]{1,0:T(8,128)S(1)}) custom-call(s32[144]{0:T(256)S(1)} %reshape.17.code_ref, bf16[8,1,128,640]{3,2,1,0:T(8,128)(2,1)S(1)} %all-to-all-done.q_hbm, bf16[5,2,128,256]{3,2,1,0:T(8,128)(2,1)} %collective-permute-done.6.refs_0_, bf16[5,2,128,256]{3,2,1,0:T(8,128)(2,1)} %collective-permute-done.7.refs_1_, ...), custom_call_target="tpu_custom_call" | custom-call | flops 3221225472 | bytes 1024 | tf_op jit(solution)/shard_map/pallas_call | solution.py:363
  109.1 6.1 %all-to-all-start.3 = ((bf16[8,128,256]{2,1,0:T(8,128)(2,1)}), bf16[8,128,256]{2,1,0:T(8,128)(2,1)S(1)}, u32[]{:S(2)}, u32[]{:S(2)}) async-start(bf16[8,128,256]{2,1,0:T(8,128)(2,1)} %copy-done), calls=%async_computation.3 | async-start | bytes 1048576 | tf_op jit(solution)/shard_map/all_to_all | solution.py:408
  115.2 11.7 %shard_map.53 = (f32[3,4,256,128]{3,2,1,0:T(8,128)S(1)}, f32[3,4,256,128]{3,2,1,0:T(8,128)S(1)}, f32[3,4,256,128]{3,2,1,0:T(8,128)S(1)}) custom-call(s32[144]{0:T(256)S(1)} %reshape.17.code_ref, bf16[8,1,128,640]{3,2,1,0:T(8,128)(2,1)S(1)} %all-to-all-done.q_hbm, bf16[8,2,128,384]{3,2,1,0:T(8,128)(2,1)} %collective-permute-done.refs_1_.refs_0_, ...), custom_call_target="tpu_custom_call" | custom-call | flops 1024 | bytes 1024 | tf_op jit(solution)/shard_map/pallas_call | solution.py:338
  126.9 6.8 %shard_map.54 = (bf16[8,128,384]{2,1,0:T(8,128)(2,1)S(1)}, f32[8,128]{1,0:T(8,128)}) custom-call(s32[144]{0:T(256)S(1)} %reshape.17.code_ref, bf16[8,1,128,640]{3,2,1,0:T(8,128)(2,1)S(1)} %all-to-all-done.q_hbm, bf16[5,2,128,384]{3,2,1,0:T(8,128)(2,1)} %collective-permute-done.4.refs_0_, bf16[5,2,128,384]{3,2,1,0:T(8,128)(2,1)} %collective-permute-done.5.refs_1_, ...), custom_call_target="tpu_custom_call" | custom-call | flops 1024 | bytes 1024 | tf_op jit(solution)/shard_map/pallas_call | solution.py:363
  133.7 15.7 %all_to_all.25.refs_1_ = bf16[8,128,384]{2,1,0:T(8,128)(2,1)S(1)} all-to-all(bf16[8,128,384]{2,1,0:T(8,128)(2,1)S(1)} %get-tuple-element.34), channel_id=1, replica_groups=mesh['groups'=1,'outer'=4,'inner'=4,'uly'=2,'rep'=1] {'inner','rep','uly'}, dimensions={0} | all-to-all | bytes 1572864 | tf_op jit(solution)/shard_map/all_to_all | solution.py:408
  (23 shorter events, 10.0 us)
Async XLA Ops:
  2.2 19.0 %all-to-all-start.2 = ((bf16[8,2,128,256]{3,2,1,0:T(8,128)(2,1)}), bf16[8,2,128,256]{3,2,1,0:T(8,128)(2,1)}, u32[]{:S(2)}, u32[]{:S(2)}) async-start(bf16[8,2,128,256]{3,2,1,0:T(8,128)(2,1)} %shard_map.48), calls=%async_computation.2 | async-start | bytes 2097152 | tf_op jit(solution)/shard_map/all_to_all | solution.py:408
  7.0 2.5 %copy-start.1 = (s32[32,16]{0,1:T(8,128)S(1)}, s32[32,16]{0,1:T(8,128)}, u32[]{:S(2)}) copy-start(s32[32,16]{0,1:T(8,128)} %param.7) | copy-start | bytes 6148
  21.2 24.2 %all-to-all-start.1 = ((bf16[8,2,128,384]{3,2,1,0:T(8,128)(2,1)}), bf16[8,2,128,384]{3,2,1,0:T(8,128)(2,1)S(1)}, u32[]{:S(2)}, u32[]{:S(2)}) async-start(bf16[8,2,128,384]{3,2,1,0:T(8,128)(2,1)} %shard_map.46.refs_1_), calls=%async_computation.1 | async-start | bytes 3145728 | tf_op jit(solution)/shard_map/all_to_all | solution.py:408
  25.5 30.5 %collective-permute-start.3 = (bf16[8,2,128,256]{3,2,1,0:T(8,128)(2,1)}, bf16[8,2,128,256]{3,2,1,0:T(8,128)(2,1)}, u32[]{:S(2)}, u32[]{:S(2)}) collective-permute-start(bf16[8,2,128,256]{3,2,1,0:T(8,128)(2,1)} %all-to-all-done.2.refs_1_), channel_id=1, source_target_pairs={{8,0},{16,8},{24,16},{9,1},{17,9},{25,17},{10,2},{18,10},{26,18},{... | collective-permute-start | bytes 3145736 | tf_op jit(solution)/shard_map/ppermute | solution.py:413
  27.6 28.4 %collective-permute-start.2 = (bf16[8,2,128,256]{3,2,1,0:T(8,128)(2,1)}, bf16[8,2,128,256]{3,2,1,0:T(8,128)(2,1)}, u32[]{:S(2)}, u32[]{:S(2)}) collective-permute-start(bf16[8,2,128,256]{3,2,1,0:T(8,128)(2,1)} %all-to-all-done.2.refs_1_), channel_id=1, source_target_pairs={{0,8},{8,16},{16,24},{1,9},{9,17},{17,25},{2,10},{10,18},{18,26},{... | collective-permute-start | bytes 3145736 | tf_op jit(solution)/shard_map/ppermute | solution.py:413
  45.4 21.2 %all-to-all-start = ((bf16[8,1,128,640]{3,2,1,0:T(8,128)(2,1)}), bf16[8,1,128,640]{3,2,1,0:T(8,128)(2,1)S(1)}, u32[]{:S(2)}, u32[]{:S(2)}) async-start(bf16[8,1,128,640]{3,2,1,0:T(8,128)(2,1)} %shard_map.47), calls=%async_computation | async-start | bytes 2621440 | tf_op jit(solution)/shard_map/all_to_all | solution.py:408
  49.6 38.0 %collective-permute-start.1 = (bf16[8,2,128,384]{3,2,1,0:T(8,128)(2,1)S(1)}, bf16[8,2,128,384]{3,2,1,0:T(8,128)(2,1)}, u32[]{:S(2)}, u32[]{:S(2)}) collective-permute-start(bf16[8,2,128,384]{3,2,1,0:T(8,128)(2,1)S(1)} %all-to-all-done.1.refs_1_), channel_id=1, source_target_pairs={{8,0},{16,8},{24,16},{9,1},{17,9},{25,17},{10,2},{18,10},{26,18},{... | collective-permute-start | bytes 4718600 | tf_op jit(solution)/shard_map/ppermute | solution.py:413
  51.7 37.7 %collective-permute-start = (bf16[8,2,128,384]{3,2,1,0:T(8,128)(2,1)S(1)}, bf16[8,2,128,384]{3,2,1,0:T(8,128)(2,1)}, u32[]{:S(2)}, u32[]{:S(2)}) collective-permute-start(bf16[8,2,128,384]{3,2,1,0:T(8,128)(2,1)S(1)} %all-to-all-done.1.refs_1_), channel_id=1, source_target_pairs={{0,8},{8,16},{16,24},{1,9},{9,17},{17,25},{2,10},{10,18},{18,26},{... | collective-permute-start | bytes 4718600 | tf_op jit(solution)/shard_map/ppermute | solution.py:413
  58.8 44.8 %collective-permute-start.6 = (bf16[5,2,128,256]{3,2,1,0:T(8,128)(2,1)}, bf16[5,2,128,256]{3,2,1,0:T(8,128)(2,1)}, u32[]{:S(2)}, u32[]{:S(2)}) collective-permute-start(bf16[5,2,128,256]{3,2,1,0:T(8,128)(2,1)} %get-tuple-element.20.refs_3_), channel_id=1, source_target_pairs={{8,16},{16,24},{9,17},{17,25},{10,18},{18,26},{11,19},{19,27},{12,... | collective-permute-start | bytes 1966088 | tf_op jit(solution)/shard_map/ppermute | solution.py:413
  61.2 42.4 %collective-permute-start.7 = (bf16[5,2,128,256]{3,2,1,0:T(8,128)(2,1)}, bf16[5,2,128,256]{3,2,1,0:T(8,128)(2,1)}, u32[]{:S(2)}, u32[]{:S(2)}) collective-permute-start(bf16[5,2,128,256]{3,2,1,0:T(8,128)(2,1)} %get-tuple-element.21.refs_4_), channel_id=1, source_target_pairs={{8,0},{16,8},{9,1},{17,9},{10,2},{18,10},{11,3},{19,11},{12,4},{20... | collective-permute-start | bytes 1966088 | tf_op jit(solution)/shard_map/ppermute | solution.py:413
  92.4 34.5 %collective-permute-start.4 = (bf16[5,2,128,384]{3,2,1,0:T(8,128)(2,1)}, bf16[5,2,128,384]{3,2,1,0:T(8,128)(2,1)}, u32[]{:S(2)}, u32[]{:S(2)}) collective-permute-start(bf16[5,2,128,384]{3,2,1,0:T(8,128)(2,1)} %get-tuple-element.25.refs_5_.refs_3_), channel_id=1, source_target_pairs={{8,16},{16,24},{9,17},{17,25},{10,18},{18,26},{11,19},{19,27},{12,... | collective-permute-start | bytes 2949128 | tf_op jit(solution)/shard_map/ppermute | solution.py:413
  96.6 30.2 %collective-permute-start.5 = (bf16[5,2,128,384]{3,2,1,0:T(8,128)(2,1)}, bf16[5,2,128,384]{3,2,1,0:T(8,128)(2,1)}, u32[]{:S(2)}, u32[]{:S(2)}) collective-permute-start(bf16[5,2,128,384]{3,2,1,0:T(8,128)(2,1)} %get-tuple-element.26.refs_6_.refs_4_), channel_id=1, source_target_pairs={{8,0},{16,8},{9,1},{17,9},{10,2},{18,10},{11,3},{19,11},{12,4},{20... | collective-permute-start | bytes 2949128 | tf_op jit(solution)/shard_map/ppermute | solution.py:413
  108.3 0.8 copy-start
  109.1 24.6 %all-to-all-start.3 = ((bf16[8,128,256]{2,1,0:T(8,128)(2,1)}), bf16[8,128,256]{2,1,0:T(8,128)(2,1)S(1)}, u32[]{:S(2)}, u32[]{:S(2)}) async-start(bf16[8,128,256]{2,1,0:T(8,128)(2,1)} %copy-done), calls=%async_computation.3 | async-start | bytes 1048576 | tf_op jit(solution)/shard_map/all_to_all | solution.py:408

commit v2 on v1

--- a/solution.py
+++ b/solution.py
@@ -12,12 +12,11 @@
 BLK = 128
 BPF = 2
 REACH = 7
-CHUNKS = (2, 3)
+CHUNKS = (3, 2)
 PACK_VMEM = 60 * 1024 * 1024
 NEAR_VMEM = 24 * 1024 * 1024
 OTHER_VMEM = 14 * 1024 * 1024
 little = dict(flops=1024, bytes_accessed=1024, transcendentals=0)
-some = dict(flops=20_000_000_000, bytes_accessed=1024, transcendentals=0)
 much = dict(flops=100_000_000_000, bytes_accessed=1024, transcendentals=0)
 
 very_low = -1e30
@@ -106,7 +105,7 @@
             pltpu.SemaphoreType.DMA((count, team_size + 1)),
         ],
         compiler_params=pltpu.CompilerParams(vmem_limit_bytes=PACK_VMEM),
-        cost_estimate=pl.CostEstimate(**some),
+        cost_estimate=pl.CostEstimate(**little),
     )(*arrays, *after)
 
 

time: 152 us -> 166 us (1.092)
  the two profiles are of different devices: /device:TPU:17 before, /device:TPU:0 now
where the time goes in v2:
time: 166 us
  Pallas kernels  45.4 us (27%)
  waiting for transfers between devices  45.3 us (27%)
  blocking collectives  38.9 us (23%)
  starting transfers between devices  28.1 us (17%)
  local copies, waits for them, and re-layouts  5.31 us (3%)
    all_to_all x2, blocking collectives, exchange(): return lax.all_to_all(array, team, split_axis=0, concat_axis=0, tiled=True)  38.9 us
    ppermute x8, waiting for transfers between devices, shifted(): return lax.ppermute(array, 'outer', route)  35.1 us
    pallas_call x2, Pallas kernels, attend_near(): pl.pallas_call(body, out_shape=[partial] * 3, in_specs=[pl.BlockSpec(memo...  20.1 us
    ppermute x8, starting transfers between devices, shifted(): return lax.ppermute(array, 'outer', route)  17.4 us
    pallas_call x2, Pallas kernels, attend_far(): pl.pallas_call(body, out_shape=[result, jax.ShapeDtypeStruct((8, 128), jn...  10.7 us
    all_to_all x3, starting transfers between devices, exchange(): return lax.all_to_all(array, team, split_axis=0, concat_axis=0, tiled=True)  10.7 us
    all_to_all x3, waiting for transfers between devices, exchange(): return lax.all_to_all(array, team, split_axis=0, concat_axis=0, tiled=True)  10.2 us
    pallas_call x3, Pallas kernels, pack(): pl.pallas_call(body, out_shape=jax.ShapeDtypeStruct((team_size, len(array...  7.03 us
  transfers between devices with their start and end apart: 11, of which 6 were waited for; matrix products, arithmetic and copies ran while one was open for 1% of the time, Pallas kernels for 21%

profile of v2, /device:TPU:0, one launch (start us, length us, event | category | flops | bytes accessed | tf_op | source)
XLA Modules:
  0.0 165.5 jit_solution(11570170180372099906)
XLA Ops:
  0.0 2.5 %shard_map.48 = bf16[8,2,128,384]{3,2,1,0:T(8,128)(2,1)} custom-call(bf16[128,5120]{1,0:T(8,128)(2,1)} %refs_0_.5, bf16[128,5120]{1,0:T(8,128)(2,1)} %refs_1_.3), custom_call_target="tpu_custom_call" | custom-call | flops 1024 | bytes 1024 | tf_op jit(solution)/shard_map/pallas_call | solution.py:98
  2.5 25.8 %all_to_all.25.refs_1_ = bf16[8,2,128,384]{3,2,1,0:T(8,128)(2,1)} all-to-all(bf16[8,2,128,384]{3,2,1,0:T(8,128)(2,1)} %shard_map.48), channel_id=1, replica_groups=mesh['groups'=1,'outer'=4,'inner'=4,'uly'=2,'rep'=1] {'inner','rep','uly'}, dimensions={0} | all-to-all | bytes 3145728 | tf_op jit(solution)/shard_map/all_to_all | solution.py:407
  28.3 5.1 %collective-permute-start.2 = (bf16[8,2,128,384]{3,2,1,0:T(8,128)(2,1)}, bf16[8,2,128,384]{3,2,1,0:T(8,128)(2,1)}, u32[]{:S(2)}, u32[]{:S(2)}) collective-permute-start(bf16[8,2,128,384]{3,2,1,0:T(8,128)(2,1)} %all_to_all.25.refs_1_), channel_id=1, source_target_pairs={{0,8},{8,16},{16,24},{1,9},{9,17},{17,25},{2,10},{10,18},{18,26},{... | collective-permute-start | bytes 4718600 | tf_op jit(solution)/shard_map/ppermute | solution.py:412
  34.6 2.2 %shard_map.46.refs_1_ = bf16[8,2,128,256]{3,2,1,0:T(8,128)(2,1)} custom-call(bf16[128,5120]{1,0:T(8,128)(2,1)} %refs_0_.5, bf16[128,5120]{1,0:T(8,128)(2,1)} %refs_1_.3), custom_call_target="tpu_custom_call" | custom-call | flops 1024 | bytes 1024 | tf_op jit(solution)/shard_map/pallas_call | solution.py:98
  36.9 3.6 %all-to-all-start.1 = ((bf16[8,2,128,256]{3,2,1,0:T(8,128)(2,1)}), bf16[8,2,128,256]{3,2,1,0:T(8,128)(2,1)S(1)}, u32[]{:S(2)}, u32[]{:S(2)}) async-start(bf16[8,2,128,256]{3,2,1,0:T(8,128)(2,1)} %shard_map.46.refs_1_), calls=%async_computation.1 | async-start | bytes 2097152 | tf_op jit(solution)/shard_map/all_to_all | solution.py:407
  40.4 2.3 %shard_map.47 = bf16[8,1,128,640]{3,2,1,0:T(8,128)(2,1)} custom-call(bf16[128,5120]{1,0:T(8,128)(2,1)} %refs_0_.4, bf16[8,2,128,256]{3,2,1,0:T(8,128)(2,1)} %shard_map.46.refs_1_), custom_call_target="tpu_custom_call" | custom-call | flops 1024 | bytes 1024 | tf_op jit(solution)/shard_map/pallas_call | solution.py:98
  45.1 10.2 %all-to-all-done.1.refs_1_ = bf16[8,2,128,256]{3,2,1,0:T(8,128)(2,1)S(1)} async-done(((bf16[8,2,128,256]{3,2,1,0:T(8,128)(2,1)}), bf16[8,2,128,256]{3,2,1,0:T(8,128)(2,1)S(1)}, u32[]{:S(2)}, u32[]{:S(2)}) %all-to-all-start.1) | async-done | bytes 1048608 | tf_op jit(solution)/shard_map/all_to_all | solution.py:407
  55.3 3.6 %all-to-all-start = ((bf16[8,1,128,640]{3,2,1,0:T(8,128)(2,1)}), bf16[8,1,128,640]{3,2,1,0:T(8,128)(2,1)S(1)}, u32[]{:S(2)}, u32[]{:S(2)}) async-start(bf16[8,1,128,640]{3,2,1,0:T(8,128)(2,1)} %shard_map.47), calls=%async_computation | async-start | bytes 2621440 | tf_op jit(solution)/shard_map/all_to_all | solution.py:407
  58.9 4.6 %collective-permute-start = (bf16[8,2,128,256]{3,2,1,0:T(8,128)(2,1)S(1)}, bf16[8,2,128,256]{3,2,1,0:T(8,128)(2,1)S(1)}, u32[]{:S(2)}, u32[]{:S(2)}) collective-permute-start(bf16[8,2,128,256]{3,2,1,0:T(8,128)(2,1)S(1)} %all-to-all-done.1.refs_1_), channel_id=1, source_target_pairs={{0,8},{8,16},{16,24},{1,9},{9,17},{17,25},{2,10},{10,18},{18,26},{... | collective-permute-start | bytes 3145736 | tf_op jit(solution)/shard_map/ppermute | solution.py:412
  64.8 2.5 %collective-permute-done.2.refs_1_.refs_0_ = bf16[8,2,128,384]{3,2,1,0:T(8,128)(2,1)} collective-permute-done((bf16[8,2,128,384]{3,2,1,0:T(8,128)(2,1)}, bf16[8,2,128,384]{3,2,1,0:T(8,128)(2,1)}, u32[]{:S(2)}, u32[]{:S(2)}) %collective-permute-start.2) | collective-permute-done | bytes 1572896 | tf_op jit(solution)/shard_map/ppermute | solution.py:412
  67.3 5.6 %collective-permute-done.3.refs_2_ = bf16[8,2,128,384]{3,2,1,0:T(8,128)(2,1)} collective-permute-done((bf16[8,2,128,384]{3,2,1,0:T(8,128)(2,1)}, bf16[8,2,128,384]{3,2,1,0:T(8,128)(2,1)}, u32[]{:S(2)}, u32[]{:S(2)}) %collective-permute-start.3) | collective-permute-done | bytes 1572896 | tf_op jit(solution)/shard_map/ppermute | solution.py:412
  72.8 3.0 %shard_map.49 = (bf16[5,2,128,384]{3,2,1,0:T(8,128)(2,1)}, bf16[5,2,128,384]{3,2,1,0:T(8,128)(2,1)}) custom-call(s32[2]{0:T(128)S(1)} %pad_add_fusion.refs_0_, bf16[8,2,128,384]{3,2,1,0:T(8,128)(2,1)} %collective-permute-done.2.refs_1_.refs_0_, bf16[8,2,128,384]{3,2,1,0:T(8,128)(2,1)} %collective-permute-done.3.refs_2_), custom_call_target="tpu_custom_call" | custom-call | flops 99999997952 | bytes 1024 | tf_op jit(solution)/shard_map/pallas_call | solution.py:52
  75.8 1.7 %collective-permute-start.6 = (bf16[5,2,128,384]{3,2,1,0:T(8,128)(2,1)}, bf16[5,2,128,384]{3,2,1,0:T(8,128)(2,1)}, u32[]{:S(2)}, u32[]{:S(2)}) collective-permute-start(bf16[5,2,128,384]{3,2,1,0:T(8,128)(2,1)} %get-tuple-element.20.refs_3_), channel_id=1, source_target_pairs={{8,16},{16,24},{9,17},{17,25},{10,18},{18,26},{11,19},{19,27},{12,... | collective-permute-start | bytes 2949128 | tf_op jit(solution)/shard_map/ppermute | solution.py:412
  78.8 11.8 %shard_map.50 = (f32[3,4,256,128]{3,2,1,0:T(8,128)S(1)}, f32[3,4,256,128]{3,2,1,0:T(8,128)S(1)}, f32[3,4,256,128]{3,2,1,0:T(8,128)S(1)}) custom-call(s32[144]{0:T(256)S(1)} %reshape.17.code_ref, bf16[8,1,128,640]{3,2,1,0:T(8,128)(2,1)S(1)} %all-to-all-done.q_hbm, bf16[8,2,128,384]{3,2,1,0:T(8,128)(2,1)} %collective-permute-done.2.refs_1_.refs_0_, ...), custom_call_target="tpu_custom_call" | custom-call | flops 15703474176 | bytes 1024 | tf_op jit(solution)/shard_map/pallas_call | solution.py:337
  90.7 4.6 %collective-permute-done.1.refs_2_ = bf16[8,2,128,256]{3,2,1,0:T(8,128)(2,1)} collective-permute-done((bf16[8,2,128,256]{3,2,1,0:T(8,128)(2,1)S(1)}, bf16[8,2,128,256]{3,2,1,0:T(8,128)(2,1)}, u32[]{:S(2)}, u32[]{:S(2)}) %collective-permute-start.1) | collective-permute-done | bytes 1048608 | tf_op jit(solution)/shard_map/ppermute | solution.py:412
  95.3 3.3 %shard_map.51 = (bf16[5,2,128,256]{3,2,1,0:T(8,128)(2,1)S(1)}, bf16[5,2,128,256]{3,2,1,0:T(8,128)(2,1)S(1)}) custom-call(s32[2]{0:T(128)S(1)} %pad_add_fusion.refs_0_, bf16[8,2,128,256]{3,2,1,0:T(8,128)(2,1)S(1)} %collective-permute-done.refs_1_.refs_0_, bf16[8,2,128,256]{3,2,1,0:T(8,128)(2,1)} %collective-permute-done.1.refs_2_, ...), custom_call_target="tpu_custom_call" | custom-call | flops 99999997952 | bytes 1024 | tf_op jit(solution)/shard_map/pallas_call | solution.py:52
  98.6 16.6 %collective-permute-done.7.refs_1_ = bf16[5,2,128,384]{3,2,1,0:T(8,128)(2,1)} collective-permute-done((bf16[5,2,128,384]{3,2,1,0:T(8,128)(2,1)}, bf16[5,2,128,384]{3,2,1,0:T(8,128)(2,1)}, u32[]{:S(2)}, u32[]{:S(2)}) %collective-permute-start.7) | collective-permute-done | bytes 983072 | tf_op jit(solution)/shard_map/ppermute | solution.py:412
  115.2 6.2 %shard_map.52 = (bf16[8,128,384]{2,1,0:T(8,128)(2,1)S(1)}, f32[8,128]{1,0:T(8,128)S(1)}) custom-call(s32[144]{0:T(256)S(1)} %reshape.17.code_ref, bf16[8,1,128,640]{3,2,1,0:T(8,128)(2,1)S(1)} %all-to-all-done.q_hbm, bf16[5,2,128,384]{3,2,1,0:T(8,128)(2,1)} %collective-permute-done.6.refs_0_, bf16[5,2,128,384]{3,2,1,0:T(8,128)(2,1)} %collective-permute-done.7.refs_1_, ...), custom_call_target="tpu_custom_call" | custom-call | flops 4831838208 | bytes 1024 | tf_op jit(solution)/shard_map/pallas_call | solution.py:362
  122.3 3.5 %all-to-all-start.3 = ((bf16[8,128,384]{2,1,0:T(8,128)(2,1)}), bf16[8,128,384]{2,1,0:T(8,128)(2,1)S(1)}, u32[]{:S(2)}, u32[]{:S(2)}) async-start(bf16[8,128,384]{2,1,0:T(8,128)(2,1)} %copy-done.2), calls=%async_computation.3 | async-start | bytes 1572864 | tf_op jit(solution)/shard_map/all_to_all | solution.py:407
  126.6 1.5 collective-permute-start.5
  131.5 8.3 %shard_map.53 = (f32[2,4,256,128]{3,2,1,0:T(8,128)S(1)}, f32[2,4,256,128]{3,2,1,0:T(8,128)S(1)}, f32[2,4,256,128]{3,2,1,0:T(8,128)S(1)}) custom-call(s32[144]{0:T(256)S(1)} %reshape.17.code_ref, bf16[8,1,128,640]{3,2,1,0:T(8,128)(2,1)S(1)} %all-to-all-done.q_hbm, bf16[8,2,128,256]{3,2,1,0:T(8,128)(2,1)S(1)} %copy-done.1, ...), custom_call_target="tpu_custom_call" | custom-call | flops 1024 | bytes 1024 | tf_op jit(solution)/shard_map/pallas_call | solution.py:337
  139.8 5.9 %collective-permute-done.5.refs_1_ = bf16[5,2,128,256]{3,2,1,0:T(8,128)(2,1)S(1)} collective-permute-done((bf16[5,2,128,256]{3,2,1,0:T(8,128)(2,1)}, bf16[5,2,128,256]{3,2,1,0:T(8,128)(2,1)S(1)}, u32[]{:S(2)}, u32[]{:S(2)}) %collective-permute-start.5) | collective-permute-done | bytes 655392 | tf_op jit(solution)/shard_map/ppermute | solution.py:412
  145.8 4.5 %shard_map.54 = (bf16[8,128,256]{2,1,0:T(8,128)(2,1)S(1)}, f32[8,128]{1,0:T(8,128)}) custom-call(s32[144]{0:T(256)S(1)} %reshape.17.code_ref, bf16[8,1,128,640]{3,2,1,0:T(8,128)(2,1)S(1)} %all-to-all-done.q_hbm, bf16[5,2,128,256]{3,2,1,0:T(8,128)(2,1)S(1)} %collective-permute-done.4.refs_0_, bf16[5,2,128,256]{3,2,1,0:T(8,128)(2,1)S(1)} %collective-permute-done.5.refs_1_, ...), custom_call_target="tpu_custom_call" | custom-call | flops 1024 | bytes 1024 | tf_op jit(solution)/shard_map/pallas_call | solution.py:362
  151.1 13.1 %all_to_all.26.refs_1_ = bf16[8,128,256]{2,1,0:T(8,128)(2,1)S(1)} all-to-all(bf16[8,128,256]{2,1,0:T(8,128)(2,1)} %copy-done.7), channel_id=1, replica_groups=mesh['groups'=1,'outer'=4,'inner'=4,'uly'=2,'rep'=1] {'inner','rep','uly'}, dimensions={0} | all-to-all | bytes 1048576 | tf_op jit(solution)/shard_map/all_to_all | solution.py:407
  (36 shorter events, 12.0 us)
Async XLA Ops:
  28.3 39.0 %collective-permute-start.2 = (bf16[8,2,128,384]{3,2,1,0:T(8,128)(2,1)}, bf16[8,2,128,384]{3,2,1,0:T(8,128)(2,1)}, u32[]{:S(2)}, u32[]{:S(2)}) collective-permute-start(bf16[8,2,128,384]{3,2,1,0:T(8,128)(2,1)} %all_to_all.25.refs_1_), channel_id=1, source_target_pairs={{0,8},{8,16},{16,24},{1,9},{9,17},{17,25},{2,10},{10,18},{18,26},{... | collective-permute-start | bytes 4718600 | tf_op jit(solution)/shard_map/ppermute | solution.py:412
  33.3 39.5 %collective-permute-start.3 = (bf16[8,2,128,384]{3,2,1,0:T(8,128)(2,1)}, bf16[8,2,128,384]{3,2,1,0:T(8,128)(2,1)}, u32[]{:S(2)}, u32[]{:S(2)}) collective-permute-start(bf16[8,2,128,384]{3,2,1,0:T(8,128)(2,1)} %all_to_all.25.refs_1_), channel_id=1, source_target_pairs={{8,0},{16,8},{24,16},{9,1},{17,9},{25,17},{10,2},{18,10},{26,18},{... | collective-permute-start | bytes 4718600 | tf_op jit(solution)/shard_map/ppermute | solution.py:412
  36.9 18.4 %all-to-all-start.1 = ((bf16[8,2,128,256]{3,2,1,0:T(8,128)(2,1)}), bf16[8,2,128,256]{3,2,1,0:T(8,128)(2,1)S(1)}, u32[]{:S(2)}, u32[]{:S(2)}) async-start(bf16[8,2,128,256]{3,2,1,0:T(8,128)(2,1)} %shard_map.46.refs_1_), calls=%async_computation.1 | async-start | bytes 2097152 | tf_op jit(solution)/shard_map/all_to_all | solution.py:407
  40.4 2.4 %copy-start.8 = (s32[32,16]{0,1:T(8,128)S(1)}, s32[32,16]{0,1:T(8,128)}, u32[]{:S(2)}) copy-start(s32[32,16]{0,1:T(8,128)} %param.7) | copy-start | bytes 6148
  55.3 23.6 %all-to-all-start = ((bf16[8,1,128,640]{3,2,1,0:T(8,128)(2,1)}), bf16[8,1,128,640]{3,2,1,0:T(8,128)(2,1)S(1)}, u32[]{:S(2)}, u32[]{:S(2)}) async-start(bf16[8,1,128,640]{3,2,1,0:T(8,128)(2,1)} %shard_map.47), calls=%async_computation | async-start | bytes 2621440 | tf_op jit(solution)/shard_map/all_to_all | solution.py:407
  58.9 31.8 %collective-permute-start = (bf16[8,2,128,256]{3,2,1,0:T(8,128)(2,1)S(1)}, bf16[8,2,128,256]{3,2,1,0:T(8,128)(2,1)S(1)}, u32[]{:S(2)}, u32[]{:S(2)}) collective-permute-start(bf16[8,2,128,256]{3,2,1,0:T(8,128)(2,1)S(1)} %all-to-all-done.1.refs_1_), channel_id=1, source_target_pairs={{0,8},{8,16},{16,24},{1,9},{9,17},{17,25},{2,10},{10,18},{18,26},{... | collective-permute-start | bytes 3145736 | tf_op jit(solution)/shard_map/ppermute | solution.py:412
  63.5 31.8 %collective-permute-start.1 = (bf16[8,2,128,256]{3,2,1,0:T(8,128)(2,1)S(1)}, bf16[8,2,128,256]{3,2,1,0:T(8,128)(2,1)}, u32[]{:S(2)}, u32[]{:S(2)}) collective-permute-start(bf16[8,2,128,256]{3,2,1,0:T(8,128)(2,1)S(1)} %all-to-all-done.1.refs_1_), channel_id=1, source_target_pairs={{8,0},{16,8},{24,16},{9,1},{17,9},{25,17},{10,2},{18,10},{26,18},{... | collective-permute-start | bytes 3145736 | tf_op jit(solution)/shard_map/ppermute | solution.py:412
  75.8 22.8 %collective-permute-start.6 = (bf16[5,2,128,384]{3,2,1,0:T(8,128)(2,1)}, bf16[5,2,128,384]{3,2,1,0:T(8,128)(2,1)}, u32[]{:S(2)}, u32[]{:S(2)}) collective-permute-start(bf16[5,2,128,384]{3,2,1,0:T(8,128)(2,1)} %get-tuple-element.20.refs_3_), channel_id=1, source_target_pairs={{8,16},{16,24},{9,17},{17,25},{10,18},{18,26},{11,19},{19,27},{12,... | collective-permute-start | bytes 2949128 | tf_op jit(solution)/shard_map/ppermute | solution.py:412
  77.5 37.7 %collective-permute-start.7 = (bf16[5,2,128,384]{3,2,1,0:T(8,128)(2,1)}, bf16[5,2,128,384]{3,2,1,0:T(8,128)(2,1)}, u32[]{:S(2)}, u32[]{:S(2)}) collective-permute-start(bf16[5,2,128,384]{3,2,1,0:T(8,128)(2,1)} %get-tuple-element.21.refs_4_), channel_id=1, source_target_pairs={{8,0},{16,8},{9,1},{17,9},{10,2},{18,10},{11,3},{19,11},{12,4},{20... | collective-permute-start | bytes 2949128 | tf_op jit(solution)/shard_map/ppermute | solution.py:412
  90.7 7.9 %copy-start = (bf16[8,2,128,256]{3,2,1,0:T(8,128)(2,1)}, bf16[8,2,128,256]{3,2,1,0:T(8,128)(2,1)S(1)}, u32[]{:S(2)}) copy-start(bf16[8,2,128,256]{3,2,1,0:T(8,128)(2,1)S(1)} %collective-permute-done.refs_1_.refs_0_) | copy-start | bytes 3145732
  98.6 22.8 %copy-start.3 = (bf16[5,2,128,256]{3,2,1,0:T(8,128)(2,1)}, bf16[5,2,128,256]{3,2,1,0:T(8,128)(2,1)S(1)}, u32[]{:S(2)}) copy-start(bf16[5,2,128,256]{3,2,1,0:T(8,128)(2,1)S(1)} %get-tuple-element.26.refs_6_.refs_4_) | copy-start | bytes 1966084
  98.6 22.8 %copy-start.5 = (bf16[5,2,128,256]{3,2,1,0:T(8,128)(2,1)}, bf16[5,2,128,256]{3,2,1,0:T(8,128)(2,1)S(1)}, u32[]{:S(2)}) copy-start(bf16[5,2,128,256]{3,2,1,0:T(8,128)(2,1)S(1)} %get-tuple-element.25.refs_5_.refs_3_) | copy-start | bytes 1966084
  121.4 0.9 copy-start.2
  122.3 28.7 %all-to-all-start.3 = ((bf16[8,128,384]{2,1,0:T(8,128)(2,1)}), bf16[8,128,384]{2,1,0:T(8,128)(2,1)S(1)}, u32[]{:S(2)}, u32[]{:S(2)}) async-start(bf16[8,128,384]{2,1,0:T(8,128)(2,1)} %copy-done.2), calls=%async_computation.3 | async-start | bytes 1572864 | tf_op jit(solution)/shard_map/all_to_all | solution.py:407
  125.9 13.9 %collective-permute-start.4 = (bf16[5,2,128,256]{3,2,1,0:T(8,128)(2,1)}, bf16[5,2,128,256]{3,2,1,0:T(8,128)(2,1)S(1)}, u32[]{:S(2)}, u32[]{:S(2)}) collective-permute-start(bf16[5,2,128,256]{3,2,1,0:T(8,128)(2,1)} %copy-done.5), channel_id=1, source_target_pairs={{8,16},{16,24},{9,17},{17,25},{10,18},{18,26},{11,19},{19,27},{12,... | collective-permute-start | bytes 1966088 | tf_op jit(solution)/shard_map/ppermute | solution.py:412
  126.6 19.2 %collective-permute-start.5 = (bf16[5,2,128,256]{3,2,1,0:T(8,128)(2,1)}, bf16[5,2,128,256]{3,2,1,0:T(8,128)(2,1)S(1)}, u32[]{:S(2)}, u32[]{:S(2)}) collective-permute-start(bf16[5,2,128,256]{3,2,1,0:T(8,128)(2,1)} %copy-done.3), channel_id=1, source_target_pairs={{8,0},{16,8},{9,1},{17,9},{10,2},{18,10},{11,3},{19,11},{12,4},{20... | collective-permute-start | bytes 1966088 | tf_op jit(solution)/shard_map/ppermute | solution.py:412
  128.1 1.2 copy-start.1
  129.3 1.1 copy-start.4
  130.4 1.1 copy-start.6
  150.3 0.8 copy-start.7

commit v3 on v1

--- a/solution.py
+++ b/solution.py
@@ -305,7 +305,14 @@
         tiles = masked_scores(queries, keys, masks)
         near_top = top_ref[head, frame]
         tops = [jnp.maximum(largest(tiles[b]), near_top[b * BLK : (b + 1) * BLK]) for b in range(BPF)]
-        mixed, totals = weighted(tiles, tops, values)
+        weights = [
+            jnp.concatenate([jnp.exp2((tile - tops[b]) * to_log2).astype(jnp.bfloat16) for tile in tiles[b]], axis=1)
+            for b in range(BPF)
+        ]
+        values = jnp.concatenate(values, axis=0)
+        values = jnp.concatenate([values, jnp.ones_like(values)], axis=1)
+        product = jnp.dot(jnp.concatenate(weights, axis=0), values, preferred_element_type=jnp.float32)
+        mixed, totals = product[:, :HD], product[:, HD:]
         shrink = jnp.exp2((near_top - jnp.concatenate(tops, axis=0)) * to_log2)
         result = (acc_ref[head, frame] * shrink + mixed) / (total_ref[head, frame] * shrink + totals)
         out_ref[pl.ds(frame * per_frame, per_frame), :, columns] = result.astype(jnp.bfloat16).reshape(

time: 152 us -> 151 us (level)
  transfers between devices with their start and end apart: 12 -> 12, of which waited for: 6 -> 6; matrix products, arithmetic and copies ran while one was open for 1% -> 1% of each run, Pallas kernels for 28% -> 27%
where the time goes in v3:
time: 151 us; the launch traced here: 149 us
  starting transfers between devices  46.5 us (31%)
  Pallas kernels  44 us (29%)
  waiting for transfers between devices  39.4 us (26%)
  blocking collectives  15.7 us (10%)
  between operations  1.53 us (1%)
    ppermute x8, starting transfers between devices, shifted(): return lax.ppermute(array, 'outer', route)  27 us
    all_to_all x4, waiting for transfers between devices, exchange(): return lax.all_to_all(array, team, split_axis=0, concat_axis=0, tiled=True)  21.1 us
    pallas_call x2, Pallas kernels, attend_near(): pl.pallas_call(body, out_shape=[partial] * 3, in_specs=[pl.BlockSpec(memo...  20.1 us
    all_to_all x4, starting transfers between devices, exchange(): return lax.all_to_all(array, team, split_axis=0, concat_axis=0, tiled=True)  19.5 us
    ppermute x8, waiting for transfers between devices, shifted(): return lax.ppermute(array, 'outer', route)  18.3 us
    all_to_all x1, blocking collectives, exchange(): return lax.all_to_all(array, team, split_axis=0, concat_axis=0, tiled=True)  15.7 us
    pallas_call x2, Pallas kernels, attend_far(): pl.pallas_call(body, out_shape=[result, jax.ShapeDtypeStruct((8, 128), jn...  9.98 us
    pallas_call x3, Pallas kernels, pack(): pl.pallas_call(body, out_shape=jax.ShapeDtypeStruct((team_size, len(array...  6.96 us
  transfers between devices with their start and end apart: 12, of which 6 were waited for; matrix products, arithmetic and copies ran while one was open for 1% of the time, Pallas kernels for 27%

profile of v3, /device:TPU:17, one launch (start us, length us, event | category | flops | bytes accessed | tf_op | source)
XLA Modules:
  0.0 149.1 jit_solution(5017886168300031867)
XLA Ops:
  0.0 2.1 %shard_map.48 = bf16[8,2,128,256]{3,2,1,0:T(8,128)(2,1)} custom-call(bf16[128,5120]{1,0:T(8,128)(2,1)} %refs_0_.5, bf16[128,5120]{1,0:T(8,128)(2,1)} %refs_1_.3), custom_call_target="tpu_custom_call" | custom-call | flops 20000000000 | bytes 1024 | tf_op jit(solution)/shard_map/pallas_call | solution.py:99
  2.2 4.8 %all-to-all-start.2 = ((bf16[8,2,128,256]{3,2,1,0:T(8,128)(2,1)}), bf16[8,2,128,256]{3,2,1,0:T(8,128)(2,1)}, u32[]{:S(2)}, u32[]{:S(2)}) async-start(bf16[8,2,128,256]{3,2,1,0:T(8,128)(2,1)} %shard_map.48), calls=%async_computation.2 | async-start | bytes 2097152 | tf_op jit(solution)/shard_map/all_to_all | solution.py:415
  7.0 2.5 %shard_map.46.refs_1_ = bf16[8,2,128,384]{3,2,1,0:T(8,128)(2,1)} custom-call(bf16[128,5120]{1,0:T(8,128)(2,1)} %refs_0_.5, bf16[128,5120]{1,0:T(8,128)(2,1)} %refs_1_.3), custom_call_target="tpu_custom_call" | custom-call | flops 20000000000 | bytes 1024 | tf_op jit(solution)/shard_map/pallas_call | solution.py:99
  12.0 9.1 %all-to-all-done.2.refs_1_ = bf16[8,2,128,256]{3,2,1,0:T(8,128)(2,1)} async-done(((bf16[8,2,128,256]{3,2,1,0:T(8,128)(2,1)}), bf16[8,2,128,256]{3,2,1,0:T(8,128)(2,1)}, u32[]{:S(2)}, u32[]{:S(2)}) %all-to-all-start.2) | async-done | bytes 1048608 | tf_op jit(solution)/shard_map/all_to_all | solution.py:415
  21.2 4.3 %all-to-all-start.1 = ((bf16[8,2,128,384]{3,2,1,0:T(8,128)(2,1)}), bf16[8,2,128,384]{3,2,1,0:T(8,128)(2,1)S(1)}, u32[]{:S(2)}, u32[]{:S(2)}) async-start(bf16[8,2,128,384]{3,2,1,0:T(8,128)(2,1)} %shard_map.46.refs_1_), calls=%async_computation.1 | async-start | bytes 3145728 | tf_op jit(solution)/shard_map/all_to_all | solution.py:415
  27.6 4.2 %collective-permute-start.2 = (bf16[8,2,128,256]{3,2,1,0:T(8,128)(2,1)}, bf16[8,2,128,256]{3,2,1,0:T(8,128)(2,1)}, u32[]{:S(2)}, u32[]{:S(2)}) collective-permute-start(bf16[8,2,128,256]{3,2,1,0:T(8,128)(2,1)} %all-to-all-done.2.refs_1_), channel_id=1, source_target_pairs={{0,8},{8,16},{16,24},{1,9},{9,17},{17,25},{2,10},{10,18},{18,26},{... | collective-permute-start | bytes 3145736 | tf_op jit(solution)/shard_map/ppermute | solution.py:420
  31.8 2.3 %shard_map.47 = bf16[8,1,128,640]{3,2,1,0:T(8,128)(2,1)} custom-call(bf16[128,5120]{1,0:T(8,128)(2,1)} %refs_0_.4, bf16[8,2,128,384]{3,2,1,0:T(8,128)(2,1)} %shard_map.46.refs_1_), custom_call_target="tpu_custom_call" | custom-call | flops 20000000000 | bytes 1024 | tf_op jit(solution)/shard_map/pallas_call | solution.py:99
  34.2 11.2 %all-to-all-done.1.refs_1_ = bf16[8,2,128,384]{3,2,1,0:T(8,128)(2,1)S(1)} async-done(((bf16[8,2,128,384]{3,2,1,0:T(8,128)(2,1)}), bf16[8,2,128,384]{3,2,1,0:T(8,128)(2,1)S(1)}, u32[]{:S(2)}, u32[]{:S(2)}) %all-to-all-start.1) | async-done | bytes 1572896 | tf_op jit(solution)/shard_map/all_to_all | solution.py:415
  45.4 4.2 %all-to-all-start = ((bf16[8,1,128,640]{3,2,1,0:T(8,128)(2,1)}), bf16[8,1,128,640]{3,2,1,0:T(8,128)(2,1)S(1)}, u32[]{:S(2)}, u32[]{:S(2)}) async-start(bf16[8,1,128,640]{3,2,1,0:T(8,128)(2,1)} %shard_map.47), calls=%async_computation | async-start | bytes 2621440 | tf_op jit(solution)/shard_map/all_to_all | solution.py:415
  51.7 4.3 %collective-permute-start = (bf16[8,2,128,384]{3,2,1,0:T(8,128)(2,1)S(1)}, bf16[8,2,128,384]{3,2,1,0:T(8,128)(2,1)}, u32[]{:S(2)}, u32[]{:S(2)}) collective-permute-start(bf16[8,2,128,384]{3,2,1,0:T(8,128)(2,1)S(1)} %all-to-all-done.1.refs_1_), channel_id=1, source_target_pairs={{0,8},{8,16},{16,24},{1,9},{9,17},{17,25},{2,10},{10,18},{18,26},{... | collective-permute-start | bytes 4718600 | tf_op jit(solution)/shard_map/ppermute | solution.py:420
  56.0 2.8 %shard_map.49 = (bf16[5,2,128,256]{3,2,1,0:T(8,128)(2,1)}, bf16[5,2,128,256]{3,2,1,0:T(8,128)(2,1)}) custom-call(s32[2]{0:T(128)S(1)} %pad_add_fusion.refs_0_, bf16[8,2,128,256]{3,2,1,0:T(8,128)(2,1)} %collective-permute-done.2.refs_1_.refs_0_, bf16[8,2,128,256]{3,2,1,0:T(8,128)(2,1)} %collective-permute-done.3.refs_2_), custom_call_target="tpu_custom_call" | custom-call | flops 99999997952 | bytes 1024 | tf_op jit(solution)/shard_map/pallas_call | solution.py:53
  58.8 2.4 %collective-permute-start.6 = (bf16[5,2,128,256]{3,2,1,0:T(8,128)(2,1)}, bf16[5,2,128,256]{3,2,1,0:T(8,128)(2,1)}, u32[]{:S(2)}, u32[]{:S(2)}) collective-permute-start(bf16[5,2,128,256]{3,2,1,0:T(8,128)(2,1)} %get-tuple-element.20.refs_3_), channel_id=1, source_target_pairs={{8,16},{16,24},{9,17},{17,25},{10,18},{18,26},{11,19},{19,27},{12,... | collective-permute-start | bytes 1966088 | tf_op jit(solution)/shard_map/ppermute | solution.py:420
  61.2 4.7 %collective-permute-start.7 = (bf16[5,2,128,256]{3,2,1,0:T(8,128)(2,1)}, bf16[5,2,128,256]{3,2,1,0:T(8,128)(2,1)}, u32[]{:S(2)}, u32[]{:S(2)}) collective-permute-start(bf16[5,2,128,256]{3,2,1,0:T(8,128)(2,1)} %get-tuple-element.21.refs_4_), channel_id=1, source_target_pairs={{8,0},{16,8},{9,1},{17,9},{10,2},{18,10},{11,3},{19,11},{12,4},{20... | collective-permute-start | bytes 1966088 | tf_op jit(solution)/shard_map/ppermute | solution.py:420
  66.6 8.5 %shard_map.50 = (f32[2,4,256,128]{3,2,1,0:T(8,128)S(1)}, f32[2,4,256,128]{3,2,1,0:T(8,128)S(1)}, f32[2,4,256,128]{3,2,1,0:T(8,128)S(1)}) custom-call(s32[144]{0:T(256)S(1)} %reshape.17.code_ref, bf16[8,1,128,640]{3,2,1,0:T(8,128)(2,1)S(1)} %all-to-all-done.q_hbm, bf16[8,2,128,256]{3,2,1,0:T(8,128)(2,1)} %collective-permute-done.2.refs_1_.refs_0_, ...), custom_call_target="tpu_custom_call" | custom-call | flops 10468982784 | bytes 1024 | tf_op jit(solution)/shard_map/pallas_call | solution.py:345
  75.1 12.5 %collective-permute-done.1.refs_2_ = bf16[8,2,128,384]{3,2,1,0:T(8,128)(2,1)} collective-permute-done((bf16[8,2,128,384]{3,2,1,0:T(8,128)(2,1)S(1)}, bf16[8,2,128,384]{3,2,1,0:T(8,128)(2,1)}, u32[]{:S(2)}, u32[]{:S(2)}) %collective-permute-start.1) | collective-permute-done | bytes 1572896 | tf_op jit(solution)/shard_map/ppermute | solution.py:420
  89.4 3.0 %shard_map.51 = (bf16[5,2,128,384]{3,2,1,0:T(8,128)(2,1)}, bf16[5,2,128,384]{3,2,1,0:T(8,128)(2,1)}) custom-call(s32[2]{0:T(128)S(1)} %pad_add_fusion.refs_0_, bf16[8,2,128,384]{3,2,1,0:T(8,128)(2,1)} %collective-permute-done.refs_1_.refs_0_, bf16[8,2,128,384]{3,2,1,0:T(8,128)(2,1)} %collective-permute-done.1.refs_2_, ...), custom_call_target="tpu_custom_call" | custom-call | flops 99999997952 | bytes 1024 | tf_op jit(solution)/shard_map/pallas_call | solution.py:53
  92.4 4.2 %collective-permute-start.4 = (bf16[5,2,128,384]{3,2,1,0:T(8,128)(2,1)}, bf16[5,2,128,384]{3,2,1,0:T(8,128)(2,1)}, u32[]{:S(2)}, u32[]{:S(2)}) collective-permute-start(bf16[5,2,128,384]{3,2,1,0:T(8,128)(2,1)} %get-tuple-element.25.refs_5_.refs_3_), channel_id=1, source_target_pairs={{8,16},{16,24},{9,17},{17,25},{10,18},{18,26},{11,19},{19,27},{12,... | collective-permute-start | bytes 2949128 | tf_op jit(solution)/shard_map/ppermute | solution.py:420
  96.6 3.0 %collective-permute-start.5 = (bf16[5,2,128,384]{3,2,1,0:T(8,128)(2,1)}, bf16[5,2,128,384]{3,2,1,0:T(8,128)(2,1)}, u32[]{:S(2)}, u32[]{:S(2)}) collective-permute-start(bf16[5,2,128,384]{3,2,1,0:T(8,128)(2,1)} %get-tuple-element.26.refs_6_.refs_4_), channel_id=1, source_target_pairs={{8,0},{16,8},{9,1},{17,9},{10,2},{18,10},{11,3},{19,11},{12,4},{20... | collective-permute-start | bytes 2949128 | tf_op jit(solution)/shard_map/ppermute | solution.py:420
  99.6 3.9 %collective-permute-done.6.refs_0_ = bf16[5,2,128,256]{3,2,1,0:T(8,128)(2,1)} collective-permute-done((bf16[5,2,128,256]{3,2,1,0:T(8,128)(2,1)}, bf16[5,2,128,256]{3,2,1,0:T(8,128)(2,1)}, u32[]{:S(2)}, u32[]{:S(2)}) %collective-permute-start.6) | collective-permute-done | bytes 655392 | tf_op jit(solution)/shard_map/ppermute | solution.py:420
  103.6 4.1 %shard_map.52 = (bf16[8,128,256]{2,1,0:T(8,128)(2,1)S(1)}, f32[8,128]{1,0:T(8,128)S(1)}) custom-call(s32[144]{0:T(256)S(1)} %reshape.17.code_ref, bf16[8,1,128,640]{3,2,1,0:T(8,128)(2,1)S(1)} %all-to-all-done.q_hbm, bf16[5,2,128,256]{3,2,1,0:T(8,128)(2,1)} %collective-permute-done.6.refs_0_, bf16[5,2,128,256]{3,2,1,0:T(8,128)(2,1)} %collective-permute-done.7.refs_1_, ...), custom_call_target="tpu_custom_call" | custom-call | flops 3221225472 | bytes 1024 | tf_op jit(solution)/shard_map/pallas_call | solution.py:370
  108.5 6.1 %all-to-all-start.3 = ((bf16[8,128,256]{2,1,0:T(8,128)(2,1)}), bf16[8,128,256]{2,1,0:T(8,128)(2,1)S(1)}, u32[]{:S(2)}, u32[]{:S(2)}) async-start(bf16[8,128,256]{2,1,0:T(8,128)(2,1)} %copy-done), calls=%async_computation.3 | async-start | bytes 1048576 | tf_op jit(solution)/shard_map/all_to_all | solution.py:415
  114.6 11.7 %shard_map.53 = (f32[3,4,256,128]{3,2,1,0:T(8,128)S(1)}, f32[3,4,256,128]{3,2,1,0:T(8,128)S(1)}, f32[3,4,256,128]{3,2,1,0:T(8,128)S(1)}) custom-call(s32[144]{0:T(256)S(1)} %reshape.17.code_ref, bf16[8,1,128,640]{3,2,1,0:T(8,128)(2,1)S(1)} %all-to-all-done.q_hbm, bf16[8,2,128,384]{3,2,1,0:T(8,128)(2,1)} %collective-permute-done.refs_1_.refs_0_, ...), custom_call_target="tpu_custom_call" | custom-call | flops 1024 | bytes 1024 | tf_op jit(solution)/shard_map/pallas_call | solution.py:345
  126.3 5.9 %shard_map.54 = (bf16[8,128,384]{2,1,0:T(8,128)(2,1)S(1)}, f32[8,128]{1,0:T(8,128)}) custom-call(s32[144]{0:T(256)S(1)} %reshape.17.code_ref, bf16[8,1,128,640]{3,2,1,0:T(8,128)(2,1)S(1)} %all-to-all-done.q_hbm, bf16[5,2,128,384]{3,2,1,0:T(8,128)(2,1)} %collective-permute-done.4.refs_0_, bf16[5,2,128,384]{3,2,1,0:T(8,128)(2,1)} %collective-permute-done.5.refs_1_, ...), custom_call_target="tpu_custom_call" | custom-call | flops 1024 | bytes 1024 | tf_op jit(solution)/shard_map/pallas_call | solution.py:370
  132.2 15.7 %all_to_all.25.refs_1_ = bf16[8,128,384]{2,1,0:T(8,128)(2,1)S(1)} all-to-all(bf16[8,128,384]{2,1,0:T(8,128)(2,1)S(1)} %get-tuple-element.34), channel_id=1, replica_groups=mesh['groups'=1,'outer'=4,'inner'=4,'uly'=2,'rep'=1] {'inner','rep','uly'}, dimensions={0} | all-to-all | bytes 1572864 | tf_op jit(solution)/shard_map/all_to_all | solution.py:415
  (23 shorter events, 10.0 us)
Async XLA Ops:
  2.2 19.0 %all-to-all-start.2 = ((bf16[8,2,128,256]{3,2,1,0:T(8,128)(2,1)}), bf16[8,2,128,256]{3,2,1,0:T(8,128)(2,1)}, u32[]{:S(2)}, u32[]{:S(2)}) async-start(bf16[8,2,128,256]{3,2,1,0:T(8,128)(2,1)} %shard_map.48), calls=%async_computation.2 | async-start | bytes 2097152 | tf_op jit(solution)/shard_map/all_to_all | solution.py:415
  7.0 2.5 %copy-start.1 = (s32[32,16]{0,1:T(8,128)S(1)}, s32[32,16]{0,1:T(8,128)}, u32[]{:S(2)}) copy-start(s32[32,16]{0,1:T(8,128)} %param.7) | copy-start | bytes 6148
  21.2 24.2 %all-to-all-start.1 = ((bf16[8,2,128,384]{3,2,1,0:T(8,128)(2,1)}), bf16[8,2,128,384]{3,2,1,0:T(8,128)(2,1)S(1)}, u32[]{:S(2)}, u32[]{:S(2)}) async-start(bf16[8,2,128,384]{3,2,1,0:T(8,128)(2,1)} %shard_map.46.refs_1_), calls=%async_computation.1 | async-start | bytes 3145728 | tf_op jit(solution)/shard_map/all_to_all | solution.py:415
  25.5 30.5 %collective-permute-start.3 = (bf16[8,2,128,256]{3,2,1,0:T(8,128)(2,1)}, bf16[8,2,128,256]{3,2,1,0:T(8,128)(2,1)}, u32[]{:S(2)}, u32[]{:S(2)}) collective-permute-start(bf16[8,2,128,256]{3,2,1,0:T(8,128)(2,1)} %all-to-all-done.2.refs_1_), channel_id=1, source_target_pairs={{8,0},{16,8},{24,16},{9,1},{17,9},{25,17},{10,2},{18,10},{26,18},{... | collective-permute-start | bytes 3145736 | tf_op jit(solution)/shard_map/ppermute | solution.py:420
  27.6 28.4 %collective-permute-start.2 = (bf16[8,2,128,256]{3,2,1,0:T(8,128)(2,1)}, bf16[8,2,128,256]{3,2,1,0:T(8,128)(2,1)}, u32[]{:S(2)}, u32[]{:S(2)}) collective-permute-start(bf16[8,2,128,256]{3,2,1,0:T(8,128)(2,1)} %all-to-all-done.2.refs_1_), channel_id=1, source_target_pairs={{0,8},{8,16},{16,24},{1,9},{9,17},{17,25},{2,10},{10,18},{18,26},{... | collective-permute-start | bytes 3145736 | tf_op jit(solution)/shard_map/ppermute | solution.py:420
  45.4 21.2 %all-to-all-start = ((bf16[8,1,128,640]{3,2,1,0:T(8,128)(2,1)}), bf16[8,1,128,640]{3,2,1,0:T(8,128)(2,1)S(1)}, u32[]{:S(2)}, u32[]{:S(2)}) async-start(bf16[8,1,128,640]{3,2,1,0:T(8,128)(2,1)} %shard_map.47), calls=%async_computation | async-start | bytes 2621440 | tf_op jit(solution)/shard_map/all_to_all | solution.py:415
  49.6 38.0 %collective-permute-start.1 = (bf16[8,2,128,384]{3,2,1,0:T(8,128)(2,1)S(1)}, bf16[8,2,128,384]{3,2,1,0:T(8,128)(2,1)}, u32[]{:S(2)}, u32[]{:S(2)}) collective-permute-start(bf16[8,2,128,384]{3,2,1,0:T(8,128)(2,1)S(1)} %all-to-all-done.1.refs_1_), channel_id=1, source_target_pairs={{8,0},{16,8},{24,16},{9,1},{17,9},{25,17},{10,2},{18,10},{26,18},{... | collective-permute-start | bytes 4718600 | tf_op jit(solution)/shard_map/ppermute | solution.py:420
  51.7 37.7 %collective-permute-start = (bf16[8,2,128,384]{3,2,1,0:T(8,128)(2,1)S(1)}, bf16[8,2,128,384]{3,2,1,0:T(8,128)(2,1)}, u32[]{:S(2)}, u32[]{:S(2)}) collective-permute-start(bf16[8,2,128,384]{3,2,1,0:T(8,128)(2,1)S(1)} %all-to-all-done.1.refs_1_), channel_id=1, source_target_pairs={{0,8},{8,16},{16,24},{1,9},{9,17},{17,25},{2,10},{10,18},{18,26},{... | collective-permute-start | bytes 4718600 | tf_op jit(solution)/shard_map/ppermute | solution.py:420
  58.8 44.8 %collective-permute-start.6 = (bf16[5,2,128,256]{3,2,1,0:T(8,128)(2,1)}, bf16[5,2,128,256]{3,2,1,0:T(8,128)(2,1)}, u32[]{:S(2)}, u32[]{:S(2)}) collective-permute-start(bf16[5,2,128,256]{3,2,1,0:T(8,128)(2,1)} %get-tuple-element.20.refs_3_), channel_id=1, source_target_pairs={{8,16},{16,24},{9,17},{17,25},{10,18},{18,26},{11,19},{19,27},{12,... | collective-permute-start | bytes 1966088 | tf_op jit(solution)/shard_map/ppermute | solution.py:420
  61.2 42.4 %collective-permute-start.7 = (bf16[5,2,128,256]{3,2,1,0:T(8,128)(2,1)}, bf16[5,2,128,256]{3,2,1,0:T(8,128)(2,1)}, u32[]{:S(2)}, u32[]{:S(2)}) collective-permute-start(bf16[5,2,128,256]{3,2,1,0:T(8,128)(2,1)} %get-tuple-element.21.refs_4_), channel_id=1, source_target_pairs={{8,0},{16,8},{9,1},{17,9},{10,2},{18,10},{11,3},{19,11},{12,4},{20... | collective-permute-start | bytes 1966088 | tf_op jit(solution)/shard_map/ppermute | solution.py:420
  92.4 33.9 %collective-permute-start.4 = (bf16[5,2,128,384]{3,2,1,0:T(8,128)(2,1)}, bf16[5,2,128,384]{3,2,1,0:T(8,128)(2,1)}, u32[]{:S(2)}, u32[]{:S(2)}) collective-permute-start(bf16[5,2,128,384]{3,2,1,0:T(8,128)(2,1)} %get-tuple-element.25.refs_5_.refs_3_), channel_id=1, source_target_pairs={{8,16},{16,24},{9,17},{17,25},{10,18},{18,26},{11,19},{19,27},{12,... | collective-permute-start | bytes 2949128 | tf_op jit(solution)/shard_map/ppermute | solution.py:420
  96.6 29.6 %collective-permute-start.5 = (bf16[5,2,128,384]{3,2,1,0:T(8,128)(2,1)}, bf16[5,2,128,384]{3,2,1,0:T(8,128)(2,1)}, u32[]{:S(2)}, u32[]{:S(2)}) collective-permute-start(bf16[5,2,128,384]{3,2,1,0:T(8,128)(2,1)} %get-tuple-element.26.refs_6_.refs_4_), channel_id=1, source_target_pairs={{8,0},{16,8},{9,1},{17,9},{10,2},{18,10},{11,3},{19,11},{12,4},{20... | collective-permute-start | bytes 2949128 | tf_op jit(solution)/shard_map/ppermute | solution.py:420
  107.7 0.8 copy-start
  108.5 23.8 %all-to-all-start.3 = ((bf16[8,128,256]{2,1,0:T(8,128)(2,1)}), bf16[8,128,256]{2,1,0:T(8,128)(2,1)S(1)}, u32[]{:S(2)}, u32[]{:S(2)}) async-start(bf16[8,128,256]{2,1,0:T(8,128)(2,1)} %copy-done), calls=%async_computation.3 | async-start | bytes 1048576 | tf_op jit(solution)/shard_map/all_to_all | solution.py:415

commit v4 on v1

--- a/solution.py
+++ b/solution.py
@@ -179,15 +179,14 @@
 
 
 def weighted(tiles, tops, values):
-    totals, weights = [], []
-    for b in range(BPF):
-        exps = [jnp.exp2((tile - tops[b]) * to_log2) for tile in tiles[b]]
-        totals.append(jnp.sum(functools.reduce(jnp.add, exps), axis=1, keepdims=True))
-        weights.append(jnp.concatenate([e.astype(jnp.bfloat16) for e in exps], axis=1))
-    mixed = jnp.dot(
-        jnp.concatenate(weights, axis=0), jnp.concatenate(values, axis=0), preferred_element_type=jnp.float32
-    )
-    return mixed, jnp.concatenate(totals, axis=0)
+    weights = [
+        jnp.concatenate([jnp.exp2((tile - tops[b]) * to_log2).astype(jnp.bfloat16) for tile in tiles[b]], axis=1)
+        for b in range(BPF)
+    ]
+    values = jnp.concatenate(values, axis=0)
+    values = jnp.concatenate([values, jnp.ones_like(values)], axis=1)
+    product = jnp.dot(jnp.concatenate(weights, axis=0), values, preferred_element_type=jnp.float32)
+    return product[:, :HD], product[:, HD:]
 
 
 def mask_of(codes):
@@ -251,7 +250,7 @@
         mixed, totals = weighted(tiles, tops, values)
         acc_ref[head, frame] = mixed
         top_ref[head, frame] = jnp.broadcast_to(jnp.concatenate(tops, axis=0), mixed.shape)
-        total_ref[head, frame] = jnp.broadcast_to(totals, mixed.shape)
+        total_ref[head, frame] = totals
 
     together = math.gcd(frames, 4)
 

time: 152 us -> 150 us (0.987)
  Pallas kernels: 45.5 us -> 41.4 us
    pallas_call x2, Pallas kernels: 20.1 us -> 17.5 us  [attend_near(): pl.pallas_call(body, out_shape=[partial] * 3, in_specs=[pl.BlockSpec(memo...]
  transfers between devices with their start and end apart: 12 -> 12, of which waited for: 6 -> 6; matrix products, arithmetic and copies ran while one was open for 1% -> 1% of each run, Pallas kernels for 28% -> 26%
where the time goes in v4:
time: 150 us; the launch traced here: 148 us
  starting transfers between devices  46.5 us (31%)
  Pallas kernels  41.4 us (28%)
  waiting for transfers between devices  40.4 us (27%)
  blocking collectives  16.4 us (11%)
  between operations  1.53 us (1%)
    ppermute x8, starting transfers between devices, shifted(): return lax.ppermute(array, 'outer', route)  27 us
    all_to_all x4, waiting for transfers between devices, exchange(): return lax.all_to_all(array, team, split_axis=0, concat_axis=0, tiled=True)  21.1 us
    all_to_all x4, starting transfers between devices, exchange(): return lax.all_to_all(array, team, split_axis=0, concat_axis=0, tiled=True)  19.5 us
    ppermute x8, waiting for transfers between devices, shifted(): return lax.ppermute(array, 'outer', route)  19.4 us
    pallas_call x2, Pallas kernels, attend_near(): pl.pallas_call(body, out_shape=[partial] * 3, in_specs=[pl.BlockSpec(memo...  17.5 us
    all_to_all x1, blocking collectives, exchange(): return lax.all_to_all(array, team, split_axis=0, concat_axis=0, tiled=True)  16.4 us
    pallas_call x2, Pallas kernels, attend_far(): pl.pallas_call(body, out_shape=[result, jax.ShapeDtypeStruct((8, 128), jn...  9.99 us
    pallas_call x3, Pallas kernels, pack(): pl.pallas_call(body, out_shape=jax.ShapeDtypeStruct((team_size, len(array...  6.96 us
  transfers between devices with their start and end apart: 12, of which 6 were waited for; matrix products, arithmetic and copies ran while one was open for 1% of the time, Pallas kernels for 26%

profile of v4, /device:TPU:17, one launch (start us, length us, event | category | flops | bytes accessed | tf_op | source)
XLA Modules:
  0.0 148.2 jit_solution(7031342930625061233)
XLA Ops:
  0.0 2.1 %shard_map.48 = bf16[8,2,128,256]{3,2,1,0:T(8,128)(2,1)} custom-call(bf16[128,5120]{1,0:T(8,128)(2,1)} %refs_0_.5, bf16[128,5120]{1,0:T(8,128)(2,1)} %refs_1_.3), custom_call_target="tpu_custom_call" | custom-call | flops 20000000000 | bytes 1024 | tf_op jit(solution)/shard_map/pallas_call | solution.py:99
  2.2 4.8 %all-to-all-start.2 = ((bf16[8,2,128,256]{3,2,1,0:T(8,128)(2,1)}), bf16[8,2,128,256]{3,2,1,0:T(8,128)(2,1)}, u32[]{:S(2)}, u32[]{:S(2)}) async-start(bf16[8,2,128,256]{3,2,1,0:T(8,128)(2,1)} %shard_map.48), calls=%async_computation.2 | async-start | bytes 2097152 | tf_op jit(solution)/shard_map/all_to_all | solution.py:407
  7.0 2.5 %shard_map.46.refs_1_ = bf16[8,2,128,384]{3,2,1,0:T(8,128)(2,1)} custom-call(bf16[128,5120]{1,0:T(8,128)(2,1)} %refs_0_.5, bf16[128,5120]{1,0:T(8,128)(2,1)} %refs_1_.3), custom_call_target="tpu_custom_call" | custom-call | flops 20000000000 | bytes 1024 | tf_op jit(solution)/shard_map/pallas_call | solution.py:99
  12.0 9.1 %all-to-all-done.2.refs_1_ = bf16[8,2,128,256]{3,2,1,0:T(8,128)(2,1)} async-done(((bf16[8,2,128,256]{3,2,1,0:T(8,128)(2,1)}), bf16[8,2,128,256]{3,2,1,0:T(8,128)(2,1)}, u32[]{:S(2)}, u32[]{:S(2)}) %all-to-all-start.2) | async-done | bytes 1048608 | tf_op jit(solution)/shard_map/all_to_all | solution.py:407
  21.2 4.3 %all-to-all-start.1 = ((bf16[8,2,128,384]{3,2,1,0:T(8,128)(2,1)}), bf16[8,2,128,384]{3,2,1,0:T(8,128)(2,1)S(1)}, u32[]{:S(2)}, u32[]{:S(2)}) async-start(bf16[8,2,128,384]{3,2,1,0:T(8,128)(2,1)} %shard_map.46.refs_1_), calls=%async_computation.1 | async-start | bytes 3145728 | tf_op jit(solution)/shard_map/all_to_all | solution.py:407
  27.6 4.2 %collective-permute-start.2 = (bf16[8,2,128,256]{3,2,1,0:T(8,128)(2,1)}, bf16[8,2,128,256]{3,2,1,0:T(8,128)(2,1)}, u32[]{:S(2)}, u32[]{:S(2)}) collective-permute-start(bf16[8,2,128,256]{3,2,1,0:T(8,128)(2,1)} %all-to-all-done.2.refs_1_), channel_id=1, source_target_pairs={{0,8},{8,16},{16,24},{1,9},{9,17},{17,25},{2,10},{10,18},{18,26},{... | collective-permute-start | bytes 3145736 | tf_op jit(solution)/shard_map/ppermute | solution.py:412
  31.8 2.3 %shard_map.47 = bf16[8,1,128,640]{3,2,1,0:T(8,128)(2,1)} custom-call(bf16[128,5120]{1,0:T(8,128)(2,1)} %refs_0_.4, bf16[8,2,128,384]{3,2,1,0:T(8,128)(2,1)} %shard_map.46.refs_1_), custom_call_target="tpu_custom_call" | custom-call | flops 20000000000 | bytes 1024 | tf_op jit(solution)/shard_map/pallas_call | solution.py:99
  34.2 11.2 %all-to-all-done.1.refs_1_ = bf16[8,2,128,384]{3,2,1,0:T(8,128)(2,1)S(1)} async-done(((bf16[8,2,128,384]{3,2,1,0:T(8,128)(2,1)}), bf16[8,2,128,384]{3,2,1,0:T(8,128)(2,1)S(1)}, u32[]{:S(2)}, u32[]{:S(2)}) %all-to-all-start.1) | async-done | bytes 1572896 | tf_op jit(solution)/shard_map/all_to_all | solution.py:407
  45.4 4.2 %all-to-all-start = ((bf16[8,1,128,640]{3,2,1,0:T(8,128)(2,1)}), bf16[8,1,128,640]{3,2,1,0:T(8,128)(2,1)S(1)}, u32[]{:S(2)}, u32[]{:S(2)}) async-start(bf16[8,1,128,640]{3,2,1,0:T(8,128)(2,1)} %shard_map.47), calls=%async_computation | async-start | bytes 2621440 | tf_op jit(solution)/shard_map/all_to_all | solution.py:407
  51.7 4.3 %collective-permute-start = (bf16[8,2,128,384]{3,2,1,0:T(8,128)(2,1)S(1)}, bf16[8,2,128,384]{3,2,1,0:T(8,128)(2,1)}, u32[]{:S(2)}, u32[]{:S(2)}) collective-permute-start(bf16[8,2,128,384]{3,2,1,0:T(8,128)(2,1)S(1)} %all-to-all-done.1.refs_1_), channel_id=1, source_target_pairs={{0,8},{8,16},{16,24},{1,9},{9,17},{17,25},{2,10},{10,18},{18,26},{... | collective-permute-start | bytes 4718600 | tf_op jit(solution)/shard_map/ppermute | solution.py:412
  56.0 2.8 %shard_map.49 = (bf16[5,2,128,256]{3,2,1,0:T(8,128)(2,1)}, bf16[5,2,128,256]{3,2,1,0:T(8,128)(2,1)}) custom-call(s32[2]{0:T(128)S(1)} %pad_add_fusion.refs_0_, bf16[8,2,128,256]{3,2,1,0:T(8,128)(2,1)} %collective-permute-done.2.refs_1_.refs_0_, bf16[8,2,128,256]{3,2,1,0:T(8,128)(2,1)} %collective-permute-done.3.refs_2_), custom_call_target="tpu_custom_call" | custom-call | flops 99999997952 | bytes 1024 | tf_op jit(solution)/shard_map/pallas_call | solution.py:53
  58.8 2.4 %collective-permute-start.6 = (bf16[5,2,128,256]{3,2,1,0:T(8,128)(2,1)}, bf16[5,2,128,256]{3,2,1,0:T(8,128)(2,1)}, u32[]{:S(2)}, u32[]{:S(2)}) collective-permute-start(bf16[5,2,128,256]{3,2,1,0:T(8,128)(2,1)} %get-tuple-element.20.refs_3_), channel_id=1, source_target_pairs={{8,16},{16,24},{9,17},{17,25},{10,18},{18,26},{11,19},{19,27},{12,... | collective-permute-start | bytes 1966088 | tf_op jit(solution)/shard_map/ppermute | solution.py:412
  61.2 4.7 %collective-permute-start.7 = (bf16[5,2,128,256]{3,2,1,0:T(8,128)(2,1)}, bf16[5,2,128,256]{3,2,1,0:T(8,128)(2,1)}, u32[]{:S(2)}, u32[]{:S(2)}) collective-permute-start(bf16[5,2,128,256]{3,2,1,0:T(8,128)(2,1)} %get-tuple-element.21.refs_4_), channel_id=1, source_target_pairs={{8,0},{16,8},{9,1},{17,9},{10,2},{18,10},{11,3},{19,11},{12,4},{20... | collective-permute-start | bytes 1966088 | tf_op jit(solution)/shard_map/ppermute | solution.py:412
  66.6 7.4 %shard_map.50 = (f32[2,4,256,128]{3,2,1,0:T(8,128)S(1)}, f32[2,4,256,128]{3,2,1,0:T(8,128)S(1)}, f32[2,4,256,128]{3,2,1,0:T(8,128)S(1)}) custom-call(s32[144]{0:T(256)S(1)} %reshape.17.code_ref, bf16[8,1,128,640]{3,2,1,0:T(8,128)(2,1)S(1)} %all-to-all-done.q_hbm, bf16[8,2,128,256]{3,2,1,0:T(8,128)(2,1)} %collective-permute-done.2.refs_1_.refs_0_, ...), custom_call_target="tpu_custom_call" | custom-call | flops 10468982784 | bytes 1024 | tf_op jit(solution)/shard_map/pallas_call | solution.py:337
  74.0 13.6 %collective-permute-done.1.refs_2_ = bf16[8,2,128,384]{3,2,1,0:T(8,128)(2,1)} collective-permute-done((bf16[8,2,128,384]{3,2,1,0:T(8,128)(2,1)S(1)}, bf16[8,2,128,384]{3,2,1,0:T(8,128)(2,1)}, u32[]{:S(2)}, u32[]{:S(2)}) %collective-permute-start.1) | collective-permute-done | bytes 1572896 | tf_op jit(solution)/shard_map/ppermute | solution.py:412
  89.4 3.0 %shard_map.51 = (bf16[5,2,128,384]{3,2,1,0:T(8,128)(2,1)}, bf16[5,2,128,384]{3,2,1,0:T(8,128)(2,1)}) custom-call(s32[2]{0:T(128)S(1)} %pad_add_fusion.refs_0_, bf16[8,2,128,384]{3,2,1,0:T(8,128)(2,1)} %collective-permute-done.refs_1_.refs_0_, bf16[8,2,128,384]{3,2,1,0:T(8,128)(2,1)} %collective-permute-done.1.refs_2_, ...), custom_call_target="tpu_custom_call" | custom-call | flops 99999997952 | bytes 1024 | tf_op jit(solution)/shard_map/pallas_call | solution.py:53
  92.4 4.2 %collective-permute-start.4 = (bf16[5,2,128,384]{3,2,1,0:T(8,128)(2,1)}, bf16[5,2,128,384]{3,2,1,0:T(8,128)(2,1)}, u32[]{:S(2)}, u32[]{:S(2)}) collective-permute-start(bf16[5,2,128,384]{3,2,1,0:T(8,128)(2,1)} %get-tuple-element.25.refs_5_.refs_3_), channel_id=1, source_target_pairs={{8,16},{16,24},{9,17},{17,25},{10,18},{18,26},{11,19},{19,27},{12,... | collective-permute-start | bytes 2949128 | tf_op jit(solution)/shard_map/ppermute | solution.py:412
  96.6 3.0 %collective-permute-start.5 = (bf16[5,2,128,384]{3,2,1,0:T(8,128)(2,1)}, bf16[5,2,128,384]{3,2,1,0:T(8,128)(2,1)}, u32[]{:S(2)}, u32[]{:S(2)}) collective-permute-start(bf16[5,2,128,384]{3,2,1,0:T(8,128)(2,1)} %get-tuple-element.26.refs_6_.refs_4_), channel_id=1, source_target_pairs={{8,0},{16,8},{9,1},{17,9},{10,2},{18,10},{11,3},{19,11},{12,4},{20... | collective-permute-start | bytes 2949128 | tf_op jit(solution)/shard_map/ppermute | solution.py:412
  99.6 3.9 %collective-permute-done.6.refs_0_ = bf16[5,2,128,256]{3,2,1,0:T(8,128)(2,1)} collective-permute-done((bf16[5,2,128,256]{3,2,1,0:T(8,128)(2,1)}, bf16[5,2,128,256]{3,2,1,0:T(8,128)(2,1)}, u32[]{:S(2)}, u32[]{:S(2)}) %collective-permute-start.6) | collective-permute-done | bytes 655392 | tf_op jit(solution)/shard_map/ppermute | solution.py:412
  103.6 4.1 %shard_map.52 = (bf16[8,128,256]{2,1,0:T(8,128)(2,1)S(1)}, f32[8,128]{1,0:T(8,128)S(1)}) custom-call(s32[144]{0:T(256)S(1)} %reshape.17.code_ref, bf16[8,1,128,640]{3,2,1,0:T(8,128)(2,1)S(1)} %all-to-all-done.q_hbm, bf16[5,2,128,256]{3,2,1,0:T(8,128)(2,1)} %collective-permute-done.6.refs_0_, bf16[5,2,128,256]{3,2,1,0:T(8,128)(2,1)} %collective-permute-done.7.refs_1_, ...), custom_call_target="tpu_custom_call" | custom-call | flops 3221225472 | bytes 1024 | tf_op jit(solution)/shard_map/pallas_call | solution.py:362
  108.5 6.1 %all-to-all-start.3 = ((bf16[8,128,256]{2,1,0:T(8,128)(2,1)}), bf16[8,128,256]{2,1,0:T(8,128)(2,1)S(1)}, u32[]{:S(2)}, u32[]{:S(2)}) async-start(bf16[8,128,256]{2,1,0:T(8,128)(2,1)} %copy-done), calls=%async_computation.3 | async-start | bytes 1048576 | tf_op jit(solution)/shard_map/all_to_all | solution.py:407
  114.6 10.1 %shard_map.53 = (f32[3,4,256,128]{3,2,1,0:T(8,128)S(1)}, f32[3,4,256,128]{3,2,1,0:T(8,128)S(1)}, f32[3,4,256,128]{3,2,1,0:T(8,128)S(1)}) custom-call(s32[144]{0:T(256)S(1)} %reshape.17.code_ref, bf16[8,1,128,640]{3,2,1,0:T(8,128)(2,1)S(1)} %all-to-all-done.q_hbm, bf16[8,2,128,384]{3,2,1,0:T(8,128)(2,1)} %collective-permute-done.refs_1_.refs_0_, ...), custom_call_target="tpu_custom_call" | custom-call | flops 1024 | bytes 1024 | tf_op jit(solution)/shard_map/pallas_call | solution.py:337
  124.7 5.9 %shard_map.54 = (bf16[8,128,384]{2,1,0:T(8,128)(2,1)S(1)}, f32[8,128]{1,0:T(8,128)}) custom-call(s32[144]{0:T(256)S(1)} %reshape.17.code_ref, bf16[8,1,128,640]{3,2,1,0:T(8,128)(2,1)S(1)} %all-to-all-done.q_hbm, bf16[5,2,128,384]{3,2,1,0:T(8,128)(2,1)} %collective-permute-done.4.refs_0_, bf16[5,2,128,384]{3,2,1,0:T(8,128)(2,1)} %collective-permute-done.5.refs_1_, ...), custom_call_target="tpu_custom_call" | custom-call | flops 1024 | bytes 1024 | tf_op jit(solution)/shard_map/pallas_call | solution.py:362
  130.7 16.4 %all_to_all.25.refs_1_ = bf16[8,128,384]{2,1,0:T(8,128)(2,1)S(1)} all-to-all(bf16[8,128,384]{2,1,0:T(8,128)(2,1)S(1)} %get-tuple-element.34), channel_id=1, replica_groups=mesh['groups'=1,'outer'=4,'inner'=4,'uly'=2,'rep'=1] {'inner','rep','uly'}, dimensions={0} | all-to-all | bytes 1572864 | tf_op jit(solution)/shard_map/all_to_all | solution.py:407
  (23 shorter events, 10.0 us)
Async XLA Ops:
  2.2 19.0 %all-to-all-start.2 = ((bf16[8,2,128,256]{3,2,1,0:T(8,128)(2,1)}), bf16[8,2,128,256]{3,2,1,0:T(8,128)(2,1)}, u32[]{:S(2)}, u32[]{:S(2)}) async-start(bf16[8,2,128,256]{3,2,1,0:T(8,128)(2,1)} %shard_map.48), calls=%async_computation.2 | async-start | bytes 2097152 | tf_op jit(solution)/shard_map/all_to_all | solution.py:407
  7.0 2.5 %copy-start.1 = (s32[32,16]{0,1:T(8,128)S(1)}, s32[32,16]{0,1:T(8,128)}, u32[]{:S(2)}) copy-start(s32[32,16]{0,1:T(8,128)} %param.7) | copy-start | bytes 6148
  21.2 24.2 %all-to-all-start.1 = ((bf16[8,2,128,384]{3,2,1,0:T(8,128)(2,1)}), bf16[8,2,128,384]{3,2,1,0:T(8,128)(2,1)S(1)}, u32[]{:S(2)}, u32[]{:S(2)}) async-start(bf16[8,2,128,384]{3,2,1,0:T(8,128)(2,1)} %shard_map.46.refs_1_), calls=%async_computation.1 | async-start | bytes 3145728 | tf_op jit(solution)/shard_map/all_to_all | solution.py:407
  25.5 30.5 %collective-permute-start.3 = (bf16[8,2,128,256]{3,2,1,0:T(8,128)(2,1)}, bf16[8,2,128,256]{3,2,1,0:T(8,128)(2,1)}, u32[]{:S(2)}, u32[]{:S(2)}) collective-permute-start(bf16[8,2,128,256]{3,2,1,0:T(8,128)(2,1)} %all-to-all-done.2.refs_1_), channel_id=1, source_target_pairs={{8,0},{16,8},{24,16},{9,1},{17,9},{25,17},{10,2},{18,10},{26,18},{... | collective-permute-start | bytes 3145736 | tf_op jit(solution)/shard_map/ppermute | solution.py:412
  27.6 28.4 %collective-permute-start.2 = (bf16[8,2,128,256]{3,2,1,0:T(8,128)(2,1)}, bf16[8,2,128,256]{3,2,1,0:T(8,128)(2,1)}, u32[]{:S(2)}, u32[]{:S(2)}) collective-permute-start(bf16[8,2,128,256]{3,2,1,0:T(8,128)(2,1)} %all-to-all-done.2.refs_1_), channel_id=1, source_target_pairs={{0,8},{8,16},{16,24},{1,9},{9,17},{17,25},{2,10},{10,18},{18,26},{... | collective-permute-start | bytes 3145736 | tf_op jit(solution)/shard_map/ppermute | solution.py:412
  45.4 21.2 %all-to-all-start = ((bf16[8,1,128,640]{3,2,1,0:T(8,128)(2,1)}), bf16[8,1,128,640]{3,2,1,0:T(8,128)(2,1)S(1)}, u32[]{:S(2)}, u32[]{:S(2)}) async-start(bf16[8,1,128,640]{3,2,1,0:T(8,128)(2,1)} %shard_map.47), calls=%async_computation | async-start | bytes 2621440 | tf_op jit(solution)/shard_map/all_to_all | solution.py:407
  49.6 38.0 %collective-permute-start.1 = (bf16[8,2,128,384]{3,2,1,0:T(8,128)(2,1)S(1)}, bf16[8,2,128,384]{3,2,1,0:T(8,128)(2,1)}, u32[]{:S(2)}, u32[]{:S(2)}) collective-permute-start(bf16[8,2,128,384]{3,2,1,0:T(8,128)(2,1)S(1)} %all-to-all-done.1.refs_1_), channel_id=1, source_target_pairs={{8,0},{16,8},{24,16},{9,1},{17,9},{25,17},{10,2},{18,10},{26,18},{... | collective-permute-start | bytes 4718600 | tf_op jit(solution)/shard_map/ppermute | solution.py:412
  51.7 37.7 %collective-permute-start = (bf16[8,2,128,384]{3,2,1,0:T(8,128)(2,1)S(1)}, bf16[8,2,128,384]{3,2,1,0:T(8,128)(2,1)}, u32[]{:S(2)}, u32[]{:S(2)}) collective-permute-start(bf16[8,2,128,384]{3,2,1,0:T(8,128)(2,1)S(1)} %all-to-all-done.1.refs_1_), channel_id=1, source_target_pairs={{0,8},{8,16},{16,24},{1,9},{9,17},{17,25},{2,10},{10,18},{18,26},{... | collective-permute-start | bytes 4718600 | tf_op jit(solution)/shard_map/ppermute | solution.py:412
  58.8 44.8 %collective-permute-start.6 = (bf16[5,2,128,256]{3,2,1,0:T(8,128)(2,1)}, bf16[5,2,128,256]{3,2,1,0:T(8,128)(2,1)}, u32[]{:S(2)}, u32[]{:S(2)}) collective-permute-start(bf16[5,2,128,256]{3,2,1,0:T(8,128)(2,1)} %get-tuple-element.20.refs_3_), channel_id=1, source_target_pairs={{8,16},{16,24},{9,17},{17,25},{10,18},{18,26},{11,19},{19,27},{12,... | collective-permute-start | bytes 1966088 | tf_op jit(solution)/shard_map/ppermute | solution.py:412
  61.2 42.4 %collective-permute-start.7 = (bf16[5,2,128,256]{3,2,1,0:T(8,128)(2,1)}, bf16[5,2,128,256]{3,2,1,0:T(8,128)(2,1)}, u32[]{:S(2)}, u32[]{:S(2)}) collective-permute-start(bf16[5,2,128,256]{3,2,1,0:T(8,128)(2,1)} %get-tuple-element.21.refs_4_), channel_id=1, source_target_pairs={{8,0},{16,8},{9,1},{17,9},{10,2},{18,10},{11,3},{19,11},{12,4},{20... | collective-permute-start | bytes 1966088 | tf_op jit(solution)/shard_map/ppermute | solution.py:412
  92.4 32.3 %collective-permute-start.4 = (bf16[5,2,128,384]{3,2,1,0:T(8,128)(2,1)}, bf16[5,2,128,384]{3,2,1,0:T(8,128)(2,1)}, u32[]{:S(2)}, u32[]{:S(2)}) collective-permute-start(bf16[5,2,128,384]{3,2,1,0:T(8,128)(2,1)} %get-tuple-element.25.refs_5_.refs_3_), channel_id=1, source_target_pairs={{8,16},{16,24},{9,17},{17,25},{10,18},{18,26},{11,19},{19,27},{12,... | collective-permute-start | bytes 2949128 | tf_op jit(solution)/shard_map/ppermute | solution.py:412
  96.6 28.1 %collective-permute-start.5 = (bf16[5,2,128,384]{3,2,1,0:T(8,128)(2,1)}, bf16[5,2,128,384]{3,2,1,0:T(8,128)(2,1)}, u32[]{:S(2)}, u32[]{:S(2)}) collective-permute-start(bf16[5,2,128,384]{3,2,1,0:T(8,128)(2,1)} %get-tuple-element.26.refs_6_.refs_4_), channel_id=1, source_target_pairs={{8,0},{16,8},{9,1},{17,9},{10,2},{18,10},{11,3},{19,11},{12,4},{20... | collective-permute-start | bytes 2949128 | tf_op jit(solution)/shard_map/ppermute | solution.py:412
  107.7 0.8 copy-start
  108.5 22.2 %all-to-all-start.3 = ((bf16[8,128,256]{2,1,0:T(8,128)(2,1)}), bf16[8,128,256]{2,1,0:T(8,128)(2,1)S(1)}, u32[]{:S(2)}, u32[]{:S(2)}) async-start(bf16[8,128,256]{2,1,0:T(8,128)(2,1)} %copy-done), calls=%async_computation.3 | async-start | bytes 1048576 | tf_op jit(solution)/shard_map/all_to_all | solution.py:407

commit v5 on v4

--- a/solution.py
+++ b/solution.py
@@ -193,7 +193,7 @@
     return [jnp.where(code > 0, 0.0, very_low).astype(jnp.float32) for code in codes]
 
 
-def each_head(heads, fetches, puts, work):
+def each_head(heads, fetches, puts, work, unrolled=False):
     for head in range(heads):
         for fetch in fetches(head):
             fetch.start()
@@ -206,7 +206,11 @@
             put.start()
         return carry
 
-    lax.fori_loop(0, heads, one_head, 0)
+    if unrolled:
+        for head in range(heads):
+            one_head(jnp.int32(head), 0)
+    else:
+        lax.fori_loop(0, heads, one_head, 0)
     for head in range(heads):
         for put in puts(head):
             put.wait()
@@ -315,7 +319,7 @@
         for frame in range(frames):
             item(frame, head)
 
-    each_head(heads, fetches, puts, work)
+    each_head(heads, fetches, puts, work, unrolled=True)
 
 
 def measured_cost(blocks):

time: 150 us -> 150 us (level)
  no operation moved by 1% of the time
where the time goes in v5:
time: 150 us; the launch traced here: 148 us
  starting transfers between devices  46.5 us (31%)
  Pallas kernels  41.3 us (28%)
  waiting for transfers between devices  40.4 us (27%)
  blocking collectives  16.4 us (11%)
  between operations  1.69 us (1%)
    ppermute x8, starting transfers between devices, shifted(): return lax.ppermute(array, 'outer', route)  27 us
    all_to_all x4, waiting for transfers between devices, exchange(): return lax.all_to_all(array, team, split_axis=0, concat_axis=0, tiled=True)  21.1 us
    all_to_all x4, starting transfers between devices, exchange(): return lax.all_to_all(array, team, split_axis=0, concat_axis=0, tiled=True)  19.5 us
    ppermute x8, waiting for transfers between devices, shifted(): return lax.ppermute(array, 'outer', route)  19.4 us
    pallas_call x2, Pallas kernels, attend_near(): pl.pallas_call(body, out_shape=[partial] * 3, in_specs=[pl.BlockSpec(memo...  17.5 us
    all_to_all x1, blocking collectives, exchange(): return lax.all_to_all(array, team, split_axis=0, concat_axis=0, tiled=True)  16.4 us
    pallas_call x2, Pallas kernels, attend_far(): pl.pallas_call(body, out_shape=[result, jax.ShapeDtypeStruct((8, 128), jn...  9.93 us
    pallas_call x3, Pallas kernels, pack(): pl.pallas_call(body, out_shape=jax.ShapeDtypeStruct((team_size, len(array...  6.96 us
  transfers between devices with their start and end apart: 12, of which 6 were waited for; matrix products, arithmetic and copies ran while one was open for 1% of the time, Pallas kernels for 26%

profile of v5, /device:TPU:17, one launch (start us, length us, event | category | flops | bytes accessed | tf_op | source)
XLA Modules:
  0.0 148.3 jit_solution(4657921284597785915)
XLA Ops:
  0.0 2.1 %shard_map.48 = bf16[8,2,128,256]{3,2,1,0:T(8,128)(2,1)} custom-call(bf16[128,5120]{1,0:T(8,128)(2,1)} %refs_0_.5, bf16[128,5120]{1,0:T(8,128)(2,1)} %refs_1_.3), custom_call_target="tpu_custom_call" | custom-call | flops 20000000000 | bytes 1024 | tf_op jit(solution)/shard_map/pallas_call | solution.py:99
  2.2 4.8 %all-to-all-start.2 = ((bf16[8,2,128,256]{3,2,1,0:T(8,128)(2,1)}), bf16[8,2,128,256]{3,2,1,0:T(8,128)(2,1)}, u32[]{:S(2)}, u32[]{:S(2)}) async-start(bf16[8,2,128,256]{3,2,1,0:T(8,128)(2,1)} %shard_map.48), calls=%async_computation.2 | async-start | bytes 2097152 | tf_op jit(solution)/shard_map/all_to_all | solution.py:411
  7.0 2.5 %shard_map.46.refs_1_ = bf16[8,2,128,384]{3,2,1,0:T(8,128)(2,1)} custom-call(bf16[128,5120]{1,0:T(8,128)(2,1)} %refs_0_.5, bf16[128,5120]{1,0:T(8,128)(2,1)} %refs_1_.3), custom_call_target="tpu_custom_call" | custom-call | flops 20000000000 | bytes 1024 | tf_op jit(solution)/shard_map/pallas_call | solution.py:99
  12.0 9.1 %all-to-all-done.2.refs_1_ = bf16[8,2,128,256]{3,2,1,0:T(8,128)(2,1)} async-done(((bf16[8,2,128,256]{3,2,1,0:T(8,128)(2,1)}), bf16[8,2,128,256]{3,2,1,0:T(8,128)(2,1)}, u32[]{:S(2)}, u32[]{:S(2)}) %all-to-all-start.2) | async-done | bytes 1048608 | tf_op jit(solution)/shard_map/all_to_all | solution.py:411
  21.2 4.3 %all-to-all-start.1 = ((bf16[8,2,128,384]{3,2,1,0:T(8,128)(2,1)}), bf16[8,2,128,384]{3,2,1,0:T(8,128)(2,1)S(1)}, u32[]{:S(2)}, u32[]{:S(2)}) async-start(bf16[8,2,128,384]{3,2,1,0:T(8,128)(2,1)} %shard_map.46.refs_1_), calls=%async_computation.1 | async-start | bytes 3145728 | tf_op jit(solution)/shard_map/all_to_all | solution.py:411
  27.6 4.2 %collective-permute-start.2 = (bf16[8,2,128,256]{3,2,1,0:T(8,128)(2,1)}, bf16[8,2,128,256]{3,2,1,0:T(8,128)(2,1)}, u32[]{:S(2)}, u32[]{:S(2)}) collective-permute-start(bf16[8,2,128,256]{3,2,1,0:T(8,128)(2,1)} %all-to-all-done.2.refs_1_), channel_id=1, source_target_pairs={{0,8},{8,16},{16,24},{1,9},{9,17},{17,25},{2,10},{10,18},{18,26},{... | collective-permute-start | bytes 3145736 | tf_op jit(solution)/shard_map/ppermute | solution.py:416
  31.8 2.3 %shard_map.47 = bf16[8,1,128,640]{3,2,1,0:T(8,128)(2,1)} custom-call(bf16[128,5120]{1,0:T(8,128)(2,1)} %refs_0_.4, bf16[8,2,128,384]{3,2,1,0:T(8,128)(2,1)} %shard_map.46.refs_1_), custom_call_target="tpu_custom_call" | custom-call | flops 20000000000 | bytes 1024 | tf_op jit(solution)/shard_map/pallas_call | solution.py:99
  34.2 11.2 %all-to-all-done.1.refs_1_ = bf16[8,2,128,384]{3,2,1,0:T(8,128)(2,1)S(1)} async-done(((bf16[8,2,128,384]{3,2,1,0:T(8,128)(2,1)}), bf16[8,2,128,384]{3,2,1,0:T(8,128)(2,1)S(1)}, u32[]{:S(2)}, u32[]{:S(2)}) %all-to-all-start.1) | async-done | bytes 1572896 | tf_op jit(solution)/shard_map/all_to_all | solution.py:411
  45.4 4.2 %all-to-all-start = ((bf16[8,1,128,640]{3,2,1,0:T(8,128)(2,1)}), bf16[8,1,128,640]{3,2,1,0:T(8,128)(2,1)S(1)}, u32[]{:S(2)}, u32[]{:S(2)}) async-start(bf16[8,1,128,640]{3,2,1,0:T(8,128)(2,1)} %shard_map.47), calls=%async_computation | async-start | bytes 2621440 | tf_op jit(solution)/shard_map/all_to_all | solution.py:411
  51.7 4.3 %collective-permute-start = (bf16[8,2,128,384]{3,2,1,0:T(8,128)(2,1)S(1)}, bf16[8,2,128,384]{3,2,1,0:T(8,128)(2,1)}, u32[]{:S(2)}, u32[]{:S(2)}) collective-permute-start(bf16[8,2,128,384]{3,2,1,0:T(8,128)(2,1)S(1)} %all-to-all-done.1.refs_1_), channel_id=1, source_target_pairs={{0,8},{8,16},{16,24},{1,9},{9,17},{17,25},{2,10},{10,18},{18,26},{... | collective-permute-start | bytes 4718600 | tf_op jit(solution)/shard_map/ppermute | solution.py:416
  56.0 2.8 %shard_map.49 = (bf16[5,2,128,256]{3,2,1,0:T(8,128)(2,1)}, bf16[5,2,128,256]{3,2,1,0:T(8,128)(2,1)}) custom-call(s32[2]{0:T(128)S(1)} %pad_add_fusion.refs_0_, bf16[8,2,128,256]{3,2,1,0:T(8,128)(2,1)} %collective-permute-done.2.refs_1_.refs_0_, bf16[8,2,128,256]{3,2,1,0:T(8,128)(2,1)} %collective-permute-done.3.refs_2_), custom_call_target="tpu_custom_call" | custom-call | flops 99999997952 | bytes 1024 | tf_op jit(solution)/shard_map/pallas_call | solution.py:53
  58.8 2.4 %collective-permute-start.6 = (bf16[5,2,128,256]{3,2,1,0:T(8,128)(2,1)}, bf16[5,2,128,256]{3,2,1,0:T(8,128)(2,1)}, u32[]{:S(2)}, u32[]{:S(2)}) collective-permute-start(bf16[5,2,128,256]{3,2,1,0:T(8,128)(2,1)} %get-tuple-element.20.refs_3_), channel_id=1, source_target_pairs={{8,16},{16,24},{9,17},{17,25},{10,18},{18,26},{11,19},{19,27},{12,... | collective-permute-start | bytes 1966088 | tf_op jit(solution)/shard_map/ppermute | solution.py:416
  61.2 4.7 %collective-permute-start.7 = (bf16[5,2,128,256]{3,2,1,0:T(8,128)(2,1)}, bf16[5,2,128,256]{3,2,1,0:T(8,128)(2,1)}, u32[]{:S(2)}, u32[]{:S(2)}) collective-permute-start(bf16[5,2,128,256]{3,2,1,0:T(8,128)(2,1)} %get-tuple-element.21.refs_4_), channel_id=1, source_target_pairs={{8,0},{16,8},{9,1},{17,9},{10,2},{18,10},{11,3},{19,11},{12,4},{20... | collective-permute-start | bytes 1966088 | tf_op jit(solution)/shard_map/ppermute | solution.py:416
  66.6 7.4 %shard_map.50 = (f32[2,4,256,128]{3,2,1,0:T(8,128)S(1)}, f32[2,4,256,128]{3,2,1,0:T(8,128)S(1)}, f32[2,4,256,128]{3,2,1,0:T(8,128)S(1)}) custom-call(s32[144]{0:T(256)S(1)} %reshape.17.code_ref, bf16[8,1,128,640]{3,2,1,0:T(8,128)(2,1)S(1)} %all-to-all-done.q_hbm, bf16[8,2,128,256]{3,2,1,0:T(8,128)(2,1)} %collective-permute-done.2.refs_1_.refs_0_, ...), custom_call_target="tpu_custom_call" | custom-call | flops 10468982784 | bytes 1024 | tf_op jit(solution)/shard_map/pallas_call | solution.py:341
  74.0 13.6 %collective-permute-done.1.refs_2_ = bf16[8,2,128,384]{3,2,1,0:T(8,128)(2,1)} collective-permute-done((bf16[8,2,128,384]{3,2,1,0:T(8,128)(2,1)S(1)}, bf16[8,2,128,384]{3,2,1,0:T(8,128)(2,1)}, u32[]{:S(2)}, u32[]{:S(2)}) %collective-permute-start.1) | collective-permute-done | bytes 1572896 | tf_op jit(solution)/shard_map/ppermute | solution.py:416
  89.4 3.0 %shard_map.51 = (bf16[5,2,128,384]{3,2,1,0:T(8,128)(2,1)}, bf16[5,2,128,384]{3,2,1,0:T(8,128)(2,1)}) custom-call(s32[2]{0:T(128)S(1)} %pad_add_fusion.refs_0_, bf16[8,2,128,384]{3,2,1,0:T(8,128)(2,1)} %collective-permute-done.refs_1_.refs_0_, bf16[8,2,128,384]{3,2,1,0:T(8,128)(2,1)} %collective-permute-done.1.refs_2_, ...), custom_call_target="tpu_custom_call" | custom-call | flops 99999997952 | bytes 1024 | tf_op jit(solution)/shard_map/pallas_call | solution.py:53
  92.4 4.2 %collective-permute-start.4 = (bf16[5,2,128,384]{3,2,1,0:T(8,128)(2,1)}, bf16[5,2,128,384]{3,2,1,0:T(8,128)(2,1)}, u32[]{:S(2)}, u32[]{:S(2)}) collective-permute-start(bf16[5,2,128,384]{3,2,1,0:T(8,128)(2,1)} %get-tuple-element.25.refs_5_.refs_3_), channel_id=1, source_target_pairs={{8,16},{16,24},{9,17},{17,25},{10,18},{18,26},{11,19},{19,27},{12,... | collective-permute-start | bytes 2949128 | tf_op jit(solution)/shard_map/ppermute | solution.py:416
  96.6 3.0 %collective-permute-start.5 = (bf16[5,2,128,384]{3,2,1,0:T(8,128)(2,1)}, bf16[5,2,128,384]{3,2,1,0:T(8,128)(2,1)}, u32[]{:S(2)}, u32[]{:S(2)}) collective-permute-start(bf16[5,2,128,384]{3,2,1,0:T(8,128)(2,1)} %get-tuple-element.26.refs_6_.refs_4_), channel_id=1, source_target_pairs={{8,0},{16,8},{9,1},{17,9},{10,2},{18,10},{11,3},{19,11},{12,4},{20... | collective-permute-start | bytes 2949128 | tf_op jit(solution)/shard_map/ppermute | solution.py:416
  99.6 3.9 %collective-permute-done.6.refs_0_ = bf16[5,2,128,256]{3,2,1,0:T(8,128)(2,1)} collective-permute-done((bf16[5,2,128,256]{3,2,1,0:T(8,128)(2,1)}, bf16[5,2,128,256]{3,2,1,0:T(8,128)(2,1)}, u32[]{:S(2)}, u32[]{:S(2)}) %collective-permute-start.6) | collective-permute-done | bytes 655392 | tf_op jit(solution)/shard_map/ppermute | solution.py:416
  103.6 4.1 %shard_map.52 = (bf16[8,128,256]{2,1,0:T(8,128)(2,1)S(1)}, f32[8,128]{1,0:T(8,128)S(1)}) custom-call(s32[144]{0:T(256)S(1)} %reshape.17.code_ref, bf16[8,1,128,640]{3,2,1,0:T(8,128)(2,1)S(1)} %all-to-all-done.q_hbm, bf16[5,2,128,256]{3,2,1,0:T(8,128)(2,1)} %collective-permute-done.6.refs_0_, bf16[5,2,128,256]{3,2,1,0:T(8,128)(2,1)} %collective-permute-done.7.refs_1_, ...), custom_call_target="tpu_custom_call" | custom-call | flops 3221225472 | bytes 1024 | tf_op jit(solution)/shard_map/pallas_call | solution.py:366
  108.5 6.1 %all-to-all-start.3 = ((bf16[8,128,256]{2,1,0:T(8,128)(2,1)}), bf16[8,128,256]{2,1,0:T(8,128)(2,1)S(1)}, u32[]{:S(2)}, u32[]{:S(2)}) async-start(bf16[8,128,256]{2,1,0:T(8,128)(2,1)} %copy-done), calls=%async_computation.3 | async-start | bytes 1048576 | tf_op jit(solution)/shard_map/all_to_all | solution.py:411
  114.6 10.1 %shard_map.53 = (f32[3,4,256,128]{3,2,1,0:T(8,128)S(1)}, f32[3,4,256,128]{3,2,1,0:T(8,128)S(1)}, f32[3,4,256,128]{3,2,1,0:T(8,128)S(1)}) custom-call(s32[144]{0:T(256)S(1)} %reshape.17.code_ref, bf16[8,1,128,640]{3,2,1,0:T(8,128)(2,1)S(1)} %all-to-all-done.q_hbm, bf16[8,2,128,384]{3,2,1,0:T(8,128)(2,1)} %collective-permute-done.refs_1_.refs_0_, ...), custom_call_target="tpu_custom_call" | custom-call | flops 1024 | bytes 1024 | tf_op jit(solution)/shard_map/pallas_call | solution.py:341
  124.7 5.9 %shard_map.54 = (bf16[8,128,384]{2,1,0:T(8,128)(2,1)S(1)}, f32[8,128]{1,0:T(8,128)}) custom-call(s32[144]{0:T(256)S(1)} %reshape.17.code_ref, bf16[8,1,128,640]{3,2,1,0:T(8,128)(2,1)S(1)} %all-to-all-done.q_hbm, bf16[5,2,128,384]{3,2,1,0:T(8,128)(2,1)} %collective-permute-done.4.refs_0_, bf16[5,2,128,384]{3,2,1,0:T(8,128)(2,1)} %collective-permute-done.5.refs_1_, ...), custom_call_target="tpu_custom_call" | custom-call | flops 1024 | bytes 1024 | tf_op jit(solution)/shard_map/pallas_call | solution.py:366
  130.6 16.4 %all_to_all.25.refs_1_ = bf16[8,128,384]{2,1,0:T(8,128)(2,1)S(1)} all-to-all(bf16[8,128,384]{2,1,0:T(8,128)(2,1)S(1)} %get-tuple-element.34), channel_id=1, replica_groups=mesh['groups'=1,'outer'=4,'inner'=4,'uly'=2,'rep'=1] {'inner','rep','uly'}, dimensions={0} | all-to-all | bytes 1572864 | tf_op jit(solution)/shard_map/all_to_all | solution.py:411
  (23 shorter events, 10.0 us)
Async XLA Ops:
  2.2 19.0 %all-to-all-start.2 = ((bf16[8,2,128,256]{3,2,1,0:T(8,128)(2,1)}), bf16[8,2,128,256]{3,2,1,0:T(8,128)(2,1)}, u32[]{:S(2)}, u32[]{:S(2)}) async-start(bf16[8,2,128,256]{3,2,1,0:T(8,128)(2,1)} %shard_map.48), calls=%async_computation.2 | async-start | bytes 2097152 | tf_op jit(solution)/shard_map/all_to_all | solution.py:411
  7.0 2.5 %copy-start.1 = (s32[32,16]{0,1:T(8,128)S(1)}, s32[32,16]{0,1:T(8,128)}, u32[]{:S(2)}) copy-start(s32[32,16]{0,1:T(8,128)} %param.7) | copy-start | bytes 6148
  21.2 24.2 %all-to-all-start.1 = ((bf16[8,2,128,384]{3,2,1,0:T(8,128)(2,1)}), bf16[8,2,128,384]{3,2,1,0:T(8,128)(2,1)S(1)}, u32[]{:S(2)}, u32[]{:S(2)}) async-start(bf16[8,2,128,384]{3,2,1,0:T(8,128)(2,1)} %shard_map.46.refs_1_), calls=%async_computation.1 | async-start | bytes 3145728 | tf_op jit(solution)/shard_map/all_to_all | solution.py:411
  25.5 30.5 %collective-permute-start.3 = (bf16[8,2,128,256]{3,2,1,0:T(8,128)(2,1)}, bf16[8,2,128,256]{3,2,1,0:T(8,128)(2,1)}, u32[]{:S(2)}, u32[]{:S(2)}) collective-permute-start(bf16[8,2,128,256]{3,2,1,0:T(8,128)(2,1)} %all-to-all-done.2.refs_1_), channel_id=1, source_target_pairs={{8,0},{16,8},{24,16},{9,1},{17,9},{25,17},{10,2},{18,10},{26,18},{... | collective-permute-start | bytes 3145736 | tf_op jit(solution)/shard_map/ppermute | solution.py:416
  27.6 28.4 %collective-permute-start.2 = (bf16[8,2,128,256]{3,2,1,0:T(8,128)(2,1)}, bf16[8,2,128,256]{3,2,1,0:T(8,128)(2,1)}, u32[]{:S(2)}, u32[]{:S(2)}) collective-permute-start(bf16[8,2,128,256]{3,2,1,0:T(8,128)(2,1)} %all-to-all-done.2.refs_1_), channel_id=1, source_target_pairs={{0,8},{8,16},{16,24},{1,9},{9,17},{17,25},{2,10},{10,18},{18,26},{... | collective-permute-start | bytes 3145736 | tf_op jit(solution)/shard_map/ppermute | solution.py:416
  45.4 21.2 %all-to-all-start = ((bf16[8,1,128,640]{3,2,1,0:T(8,128)(2,1)}), bf16[8,1,128,640]{3,2,1,0:T(8,128)(2,1)S(1)}, u32[]{:S(2)}, u32[]{:S(2)}) async-start(bf16[8,1,128,640]{3,2,1,0:T(8,128)(2,1)} %shard_map.47), calls=%async_computation | async-start | bytes 2621440 | tf_op jit(solution)/shard_map/all_to_all | solution.py:411
  49.6 38.0 %collective-permute-start.1 = (bf16[8,2,128,384]{3,2,1,0:T(8,128)(2,1)S(1)}, bf16[8,2,128,384]{3,2,1,0:T(8,128)(2,1)}, u32[]{:S(2)}, u32[]{:S(2)}) collective-permute-start(bf16[8,2,128,384]{3,2,1,0:T(8,128)(2,1)S(1)} %all-to-all-done.1.refs_1_), channel_id=1, source_target_pairs={{8,0},{16,8},{24,16},{9,1},{17,9},{25,17},{10,2},{18,10},{26,18},{... | collective-permute-start | bytes 4718600 | tf_op jit(solution)/shard_map/ppermute | solution.py:416
  51.7 37.7 %collective-permute-start = (bf16[8,2,128,384]{3,2,1,0:T(8,128)(2,1)S(1)}, bf16[8,2,128,384]{3,2,1,0:T(8,128)(2,1)}, u32[]{:S(2)}, u32[]{:S(2)}) collective-permute-start(bf16[8,2,128,384]{3,2,1,0:T(8,128)(2,1)S(1)} %all-to-all-done.1.refs_1_), channel_id=1, source_target_pairs={{0,8},{8,16},{16,24},{1,9},{9,17},{17,25},{2,10},{10,18},{18,26},{... | collective-permute-start | bytes 4718600 | tf_op jit(solution)/shard_map/ppermute | solution.py:416
  58.8 44.8 %collective-permute-start.6 = (bf16[5,2,128,256]{3,2,1,0:T(8,128)(2,1)}, bf16[5,2,128,256]{3,2,1,0:T(8,128)(2,1)}, u32[]{:S(2)}, u32[]{:S(2)}) collective-permute-start(bf16[5,2,128,256]{3,2,1,0:T(8,128)(2,1)} %get-tuple-element.20.refs_3_), channel_id=1, source_target_pairs={{8,16},{16,24},{9,17},{17,25},{10,18},{18,26},{11,19},{19,27},{12,... | collective-permute-start | bytes 1966088 | tf_op jit(solution)/shard_map/ppermute | solution.py:416
  61.2 42.4 %collective-permute-start.7 = (bf16[5,2,128,256]{3,2,1,0:T(8,128)(2,1)}, bf16[5,2,128,256]{3,2,1,0:T(8,128)(2,1)}, u32[]{:S(2)}, u32[]{:S(2)}) collective-permute-start(bf16[5,2,128,256]{3,2,1,0:T(8,128)(2,1)} %get-tuple-element.21.refs_4_), channel_id=1, source_target_pairs={{8,0},{16,8},{9,1},{17,9},{10,2},{18,10},{11,3},{19,11},{12,4},{20... | collective-permute-start | bytes 1966088 | tf_op jit(solution)/shard_map/ppermute | solution.py:416
  92.4 32.3 %collective-permute-start.4 = (bf16[5,2,128,384]{3,2,1,0:T(8,128)(2,1)}, bf16[5,2,128,384]{3,2,1,0:T(8,128)(2,1)}, u32[]{:S(2)}, u32[]{:S(2)}) collective-permute-start(bf16[5,2,128,384]{3,2,1,0:T(8,128)(2,1)} %get-tuple-element.25.refs_5_.refs_3_), channel_id=1, source_target_pairs={{8,16},{16,24},{9,17},{17,25},{10,18},{18,26},{11,19},{19,27},{12,... | collective-permute-start | bytes 2949128 | tf_op jit(solution)/shard_map/ppermute | solution.py:416
  96.6 28.1 %collective-permute-start.5 = (bf16[5,2,128,384]{3,2,1,0:T(8,128)(2,1)}, bf16[5,2,128,384]{3,2,1,0:T(8,128)(2,1)}, u32[]{:S(2)}, u32[]{:S(2)}) collective-permute-start(bf16[5,2,128,384]{3,2,1,0:T(8,128)(2,1)} %get-tuple-element.26.refs_6_.refs_4_), channel_id=1, source_target_pairs={{8,0},{16,8},{9,1},{17,9},{10,2},{18,10},{11,3},{19,11},{12,4},{20... | collective-permute-start | bytes 2949128 | tf_op jit(solution)/shard_map/ppermute | solution.py:416
  107.6 0.8 copy-start
  108.5 22.1 %all-to-all-start.3 = ((bf16[8,128,256]{2,1,0:T(8,128)(2,1)}), bf16[8,128,256]{2,1,0:T(8,128)(2,1)S(1)}, u32[]{:S(2)}, u32[]{:S(2)}) async-start(bf16[8,128,256]{2,1,0:T(8,128)(2,1)} %copy-done), calls=%async_computation.3 | async-start | bytes 1048576 | tf_op jit(solution)/shard_map/all_to_all | solution.py:411
